TPU v7x, 512 devices: a whole 4x8x8 slice. The times are simulated.
512 devices in a mesh: lat: 16 (over y_hi, z), lon: 32 (over y_lo, x, core).
Axes of the slice: x: 4, y: 8 (y_hi: 2, y_lo: 4; y = y_hi * 4 + y_lo), z: 8, core: 2. Of those that a mesh axis runs over, the one named last changes fastest.
Arguments:
- grad_out: float32 [160, 720, 1440], P('lon', 'lat'), may hold values from -6 to 6
- saved_spectra: float32 [720, 96, 2, 160], P('lat', 'lon'), may hold values from -0.4375 to 0.4375
- spec_weight: float32 [720, 2, 160], replicated, may hold values from -6 to 6
- legendre: float32 [96, 720, 720], P('lon', 'lat'), may hold values from -0.3125 to 0.3125
- lat_weight: float32 [720], P('lat'), may hold values from 0.25 to 1.75
Outputs:
- grad_in: float32 [160, 720, 1440], P('lon', 'lat')
- grad_weight: float32 [720, 2, 160], P('lat')
All inputs are finite; a program needn't handle non-finite values.
Results may differ from a plain program's by a relative error of at most 0.000071.
Values sent between devices are 32-bit elements; how exact they have to be, the bound alone decides.
No kernel may reach another device: no remote copies, remote signals or barrier semaphores. Data moves between devices by JAX's collectives and lax.ppermute only.
A program may use at most 64 MiB of HBM per device.

v0:
```python
import math

import jax
import jax.numpy as jnp
from jax import lax
from jax.sharding import PartitionSpec as P


def wave_tables(orders, points):
    order_ids = jnp.arange(orders, dtype=jnp.int32)
    point_ids = jnp.arange(points, dtype=jnp.int32)
    phase = order_ids[:, None] * point_ids[None, :] % points
    angle_grid = 2.0 * math.pi / points * phase.astype(jnp.float32)
    return (jnp.cos(angle_grid), jnp.sin(angle_grid))


def conj_times(first, second):
    real_first = first[..., 0, :]
    imag_first = first[..., 1, :]
    real_second = second[..., 0, :]
    imag_second = second[..., 1, :]
    real_part = real_first * real_second + imag_first * imag_second
    imag_part = real_first * imag_second - imag_first * real_second
    return jnp.stack([real_part, imag_part], axis=-2)


def local(grad_out, saved_spectra, spec_weight, legendre, lat_weight):
    group_size, lat_rows, points = grad_out.shape
    local_orders = legendre.shape[0]
    orders = local_orders * lax.axis_size("lon")
    row_count = saved_spectra.shape[0]
    cosine, sine = wave_tables(orders, points)
    norm_factor = 1.0 / math.sqrt(points)
    forward_table = jnp.concatenate([cosine, -sine], axis=0).T * norm_factor
    coeffs = jnp.dot(
        grad_out.reshape(group_size * lat_rows, points),
        forward_table,
        precision=lax.Precision.HIGHEST,
        preferred_element_type=jnp.float32,
    )
    coeffs = coeffs.reshape(group_size, lat_rows, 2, orders)
    by_order = lax.all_to_all(coeffs, "lon", split_axis=3, concat_axis=0, tiled=True)
    row_start = lax.axis_index("lat") * row_count
    partial_terms = jnp.einsum(
        "ipl,cpri->lirc", legendre, by_order, precision=lax.Precision.HIGHEST
    )
    spectra = lax.psum(partial_terms, "lat")
    own_rows = lax.dynamic_slice_in_dim(spectra, row_start, row_count, 0)
    adjoint = conj_times(spec_weight[:, None], spectra)
    synthesis = jnp.einsum("ipl,lirc->cpri", legendre, adjoint, precision=lax.Precision.HIGHEST)
    weight_part = jnp.sum(conj_times(saved_spectra, own_rows), axis=1)
    grad_weight = lax.psum(weight_part, "lon")
    synthesis = synthesis * lat_weight[None, :, None, None]
    order_ids = jnp.arange(orders, dtype=jnp.int32)
    doubling = jnp.where(order_ids == 0, 1.0, 2.0).astype(jnp.float32)
    inverse_table = (
        jnp.concatenate([cosine * doubling[:, None], -sine * doubling[:, None]], axis=0)
        * norm_factor
    )
    block = lax.all_to_all(synthesis, "lon", split_axis=0, concat_axis=3, tiled=True)
    flat_rows = block.reshape(block.shape[0] * block.shape[1], 2 * orders)
    result = jnp.dot(
        flat_rows,
        inverse_table,
        precision=lax.Precision.HIGHEST,
        preferred_element_type=jnp.float32,
    )
    grad_in = result.reshape(block.shape[0], block.shape[1], points)
    return (grad_in, grad_weight)


def solution(mesh):
    return jax.shard_map(
        local,
        mesh=mesh,
        in_specs=(
            P("lon", "lat", None),
            P("lat", "lon", None, None),
            P(),
            P("lon", "lat", None),
            P("lat"),
        ),
        out_specs=(P("lon", "lat", None), P("lat", None, None)),
        check_vma=False,
    )
```

profile of v0, /device:TPU:1, one launch (start us, length us, event | category | flops | bytes accessed | tf_op | source)
XLA Modules:
  0.0 425.9 jit_solution(3268187368279177558)
XLA Ops:
  7.2 0.0 copy-start
  7.2 0.0 all-reduce.2.cloned.1.call-start
  7.2 2.4 sine_negate_fusion
  9.7 1.5 reshape.23
  11.2 1.5 fusion.18
  12.8 0.1 copy.39
  12.9 0.2 reshape.24
  13.1 0.3 copy.40
  13.4 0.6 reshape.27
  14.1 18.9 %all_to_all.33 = f32[32,1,1350]{2,1,0:T(1,128)S(1)} all-to-all(f32[32,1,1350]{2,1,0:T(1,128)S(1)} %reshape.27), channel_id=1, replica_groups=mesh['lat'=16,'lon'=32] {'lon'}, dimensions={0} | all-to-all | bytes 345600 | tf_op jit(solution)/shard_map/all_to_all | solution.py:42
  33.0 0.5 broadcast.22
  33.5 1.0 reduce
  34.5 0.4 reshape.28
  34.9 0.2 copy.42
  35.1 0.0 copy-done
  35.1 4.1 convolution_bitcast_fusion
  39.2 0.0 copy-start.1
  39.2 0.0 all-reduce.2.cloned.1.call-update
  39.2 1.2 copy-done.1
  40.4 0.1 slice_bitcast_fusion.1
  40.4 2.5 broadcast_multiply_fusion.1
  42.9 219.0 %all-reduce.2.cloned.1.call-done = f32[720,3,2,160]{0,3,2,1:T(8,128)} async-done(((f32[720,3,2,160]{0,3,2,1:T(8,128)}), f32[720,3,2,160]{0,3,2,1:T(8,128)}) %all-reduce.2.cloned.1.call-update) | async-done | bytes 2764816 | tf_op jit(solution)/shard_map/psum | solution.py:47
  261.9 0.0 copy-start.3
  261.9 2.1 multiply_add_fusion
  264.1 0.0 copy-done.3
  264.1 3.1 fusion.15
  267.2 0.0 copy-start.2
  267.2 0.3 copy.44
  267.6 1.3 reshape.29
  268.9 8.7 %all-to-all-start.1 = ((f32[32,1,1350]{2,1,0:T(1,128)}), f32[32,1,1350]{2,1,0:T(1,128)S(1)}, u32[]{:S(2)}, u32[]{:S(2)}) async-start(f32[32,1,1350]{2,1,0:T(1,128)} %reshape.29), calls=%async_computation.1 | async-start | bytes 360448 | tf_op jit(solution)/shard_map/all_to_all | solution.py:60
  277.5 0.0 copy-done.2
  277.5 0.2 fusion.35
  277.8 0.2 copy.54
  277.9 0.2 copy.53
  278.1 1.4 multiply_add_fusion.1
  279.6 134.4 %psum.15 = f32[45,2,160]{0,2,1:T(8,128)S(1)} all-reduce(f32[45,2,160]{0,2,1:T(8,128)S(1)} %maximum_reduce_fusion), channel_id=1, replica_groups=mesh['lat'=16,'lon'=32] {'lon'}, use_global_device_ids=true, to_apply=%region_2.3 | all-reduce | flops 14400 | bytes 115200 | tf_op jit(solution)/shard_map/psum | solution.py:52
  413.9 0.8 copy.49
  414.7 0.0 all-to-all-done.1
  414.7 1.0 reduce.1
  415.7 0.4 reshape.30
  416.1 0.2 copy.45
  416.3 0.2 dot_general.20
  416.5 2.6 fusion.8
  (2 shorter events, 0.1 us)
Async XLA Ops:
  7.2 27.9 %copy-start = (f32[3,45,720]{2,1,0:T(8,128)S(1)}, f32[3,45,720]{2,1,0:T(8,128)}, u32[]{:S(2)}) copy-start(f32[3,45,720]{2,1,0:T(8,128)} %param.8) | copy-start | bytes 1166404
  7.2 254.7 %all-reduce.2.cloned.1.call-start = ((), (), s32[]{:S(2)}) async-start(), calls=%async_computation.2 | async-start | bytes 5898240 | tf_op jit(solution)/shard_map/psum | solution.py:47
  39.2 1.2 copy-start.1
  261.9 2.2 copy-start.3
  267.2 10.3 %copy-start.2 = (f32[45,3,2,160]{3,2,1,0:T(2,128)S(1)}, f32[45,3,2,160]{3,2,1,0:T(2,128)}, u32[]{:S(2)}) copy-start(f32[45,3,2,160]{3,2,1,0:T(2,128)} %param.6) | copy-start | bytes 518404
  268.9 145.8 %all-to-all-start.1 = ((f32[32,1,1350]{2,1,0:T(1,128)}), f32[32,1,1350]{2,1,0:T(1,128)S(1)}, u32[]{:S(2)}, u32[]{:S(2)}) async-start(f32[32,1,1350]{2,1,0:T(1,128)} %reshape.29), calls=%async_computation.1 | async-start | bytes 360448 | tf_op jit(solution)/shard_map/all_to_all | solution.py:60
Sparse Core Ops, SparseCore 0:
  39.3 222.5 all-reduce.1
where the time goes:
time: 429 us; the launch traced here: 426 us
  waiting for transfers between devices  219 us (51%)
  blocking collectives  153 us (36%)
  between operations  14.3 us (3%)
  matrix products  11.3 us (3%)
  other arithmetic  10.5 us (2%)
  local copies, waits for them, and re-layouts  8.86 us (2%)
  starting transfers between devices  8.69 us (2%)
    psum x1, waiting for transfers between devices, local(): spectra = lax.psum(partial_terms, 'lat')  219 us
    psum x1, blocking collectives, local(): grad_weight = lax.psum(weight_part, 'lon')  134 us
    all_to_all x1, blocking collectives, local(): lax.all_to_all(coeffs, 'lon', split_axis=3, concat_axis=0, tiled=True)  18.9 us
    all_to_all x1, starting transfers between devices, local(): lax.all_to_all(synthesis, 'lon', split_axis=0, concat_axis=3, tiled=True)  8.65 us
  transfers between devices with their start and end apart: 2, of which 1 were waited for; matrix products, arithmetic and copies ran while one was open for 1% of the time, Pallas kernels for 0%

commit v1 on v0

v1 whole, which is shorter than its diff:
```python
import math

import jax
import jax.numpy as jnp
import numpy as np
from jax import lax
from jax.sharding import Mesh, PartitionSpec as P

NAMES = ("yh", "z", "yl", "xh", "xl", "c")
SIZES = (2, 8, 4, 2, 2, 2)
LAT = ("yh", "z")
LON = ("yl", "xh", "xl", "c")
GROUP = ("yh", "z", "yl", "xh")
HIGH = lax.Precision.HIGH
EXACT = lax.Precision.HIGHEST


def order_of(yh, z, yl, xh, xl):
    xl_o = np.where(z < 3, xl, 1 - xl)
    m = 3 * (((yl * 2 + xh) * 2 + xl_o) * 2 + yh) + z % 3
    return np.where(z < 6, m, -1)


def tables(points):
    yh, z, yl, xh = np.meshgrid(*[np.arange(n) for n in SIZES[:4]], indexing="ij")
    out = []
    for xl in range(2):
        m = order_of(yh, z, yl, xh, xl).reshape(-1)
        phase = (m[:, None] * np.arange(points)[None]) % points
        angle = 2.0 * math.pi / points * phase
        rows = np.stack([np.cos(angle), -np.sin(angle)]) / math.sqrt(points)
        out.append(np.where(m[None, :, None] >= 0, rows, 0.0))
    return np.stack(out).astype(np.float32)


def channel_picks(channels):
    per = channels // 32
    picks = np.zeros((2, channels, channels), np.float32)
    for xl in range(2):
        slot = 0
        for region in (xl, 1 - xl):
            for c in range(2):
                for yl in range(4):
                    for xh in range(2):
                        for j in range(per):
                            b = ((yl * 2 + xh) * 2 + region) * 2 + c
                            picks[xl, b * per + j, slot] = 1.0
                            slot += 1
    return picks


def local(grad_out, saved_spectra, spec_weight, legendre, lat_weight):
    group, rows, points = grad_out.shape
    degrees, _, channels = spec_weight.shape
    orders = legendre.shape[0]
    pad = -rows % 8
    wide = rows + pad
    xl, c = lax.axis_index("xl"), lax.axis_index("c")
    half, quarter = channels // 2, channels // 4

    picks = jnp.asarray(channel_picks(channels))[xl]
    sv = jnp.dot(saved_spectra.reshape(-1, channels), picks, precision=EXACT)
    sv = sv.reshape(rows, orders, 2, 2, half).transpose(3, 1, 0, 2, 4).reshape(2, orders, rows, 2 * half)
    own = jnp.concatenate([legendre, sv[0]], axis=-1)
    other = jnp.concatenate([legendre, sv[1]], axis=-1)
    own = lax.ppermute(own, ("yh", "c"), [(a * 2 + b, b * 2 + a) for a in range(2) for b in range(2)])
    other = lax.ppermute(
        other,
        ("yh", "xl", "c"),
        [(a * 4 + x * 2 + b, b * 4 + (1 - x) * 2 + a) for a in range(2) for x in range(2) for b in range(2)],
    )

    table = jnp.asarray(tables(points))[xl]
    field = jnp.pad(grad_out, ((0, 0), (0, pad), (0, 0))).reshape(group * wide, points)
    coeffs = jnp.einsum("rmx,qx->mrq", table, field, precision=HIGH)
    coeffs = jnp.pad(coeffs.reshape(128, 2 * group * wide), ((0, 0), (0, 512 - 2 * group * wide)))
    coeffs = lax.all_to_all(coeffs.reshape(128, 4, 128), GROUP, 0, 0, tiled=True)

    sent = jnp.concatenate([own, other, own[:2]], axis=0)
    sent, coeffs = lax.optimization_barrier((sent, coeffs))
    got = lax.all_to_all(sent, ("z",), 0, 0, tiled=True)
    got = lax.all_to_all(jnp.stack([got, got]), ("c",), 0, 0, tiled=True)
    got = got.reshape(16, rows, degrees + 2 * half)
    leg = jnp.pad(got[..., :degrees], ((0, 0), (0, pad), (0, 0))).reshape(16 * wide, degrees)
    sv = got[..., degrees:].reshape(degrees, 2, 2, quarter)
    sv = jnp.where(c == 0, sv[:, :, 0], sv[:, :, 1]).transpose(1, 2, 0)

    coeffs = coeffs.reshape(128, 512)[:, : 2 * group * wide].reshape(16, 8, 2, group, wide)
    coeffs = coeffs.transpose(2, 1, 3, 0, 4).reshape(2, quarter, 16 * wide)
    spectra = jnp.einsum("rhp,pl->rhl", coeffs, leg, precision=HIGH)
    weight = jnp.dot(spec_weight.reshape(-1, channels), picks[:, :half], precision=EXACT)
    weight = weight.reshape(degrees, 2, 2, quarter)
    weight = jnp.where(c == 0, weight[:, :, 0], weight[:, :, 1]).transpose(1, 2, 0)

    def conj_times(first, second):
        return jnp.stack(
            [first[0] * second[0] + first[1] * second[1], first[0] * second[1] - first[1] * second[0]]
        )

    yh, z, yl, xh = (lax.axis_index(n) for n in GROUP)
    first = (yl + xh + yh == 0) & (z == 3 * xl)
    twice = jnp.where(first, 1.0, 2.0)
    part = conj_times(sv, spectra)
    adjoint = conj_times(weight, spectra) * twice
    synthesis = jnp.einsum("rhl,pl->rhp", adjoint, leg, precision=HIGH)

    synthesis = synthesis.reshape(2, 8, group, 16, wide)
    part = jnp.pad(part.reshape(2, 8, group, 16, rows), ((0, 0),) * 4 + ((0, pad),))
    back = jnp.stack([synthesis, part]).transpose(4, 2, 0, 1, 3, 5).reshape(128, 4 * group * wide)
    back = jnp.pad(back, ((0, 0), (0, 1024 - 4 * group * wide))).reshape(128, 8, 128)
    back = lax.all_to_all(back, GROUP, 0, 0, tiled=True)
    back = back.reshape(128, 1024)[:, : 4 * group * wide].reshape(128, 2, 2, group * wide)

    share = jnp.sum(back[:, 1], axis=0).reshape(2 * group * wide)
    share = jnp.pad(share, (0, 512 - 2 * group * wide)).reshape(1, 4, 128)
    share = lax.all_to_all(jnp.broadcast_to(share, (32, 4, 128)), LON, 0, 0, tiled=True)
    grad_weight = share.reshape(32, 512)[:, : 2 * group * wide].reshape(32, 2, group, wide)[..., :rows]
    grad_weight = grad_weight.transpose(3, 1, 0, 2).reshape(rows, 2, channels)

    grad_in = jnp.einsum("mrq,rmx->qx", back[:, 0], table, precision=HIGH)
    grad_in = grad_in.reshape(group, wide, points)[:, :rows] * lat_weight[None, :, None]
    return (grad_in, grad_weight)


def solution(mesh):
    fine = Mesh(mesh.devices.reshape(SIZES), NAMES)
    return jax.shard_map(
        local,
        mesh=fine,
        in_specs=(P(LON, LAT, None), P(LAT, LON, None, None), P(), P(LON, LAT, None), P(LAT)),
        out_specs=(P(LON, LAT, None), P(LAT, None, None)),
        check_vma=False,
    )
```

time: 429 us -> 170 us (0.40)
  waiting for transfers between devices: 219 us -> 46.7 us
  blocking collectives: 153 us -> 35.6 us
  starting transfers between devices: 8.69 us -> 39.6 us
  local copies, waits for them, and re-layouts: 8.86 us -> 31.2 us
  between operations: 14.3 us -> 1.19 us
    psum x1 -> x0, waiting for transfers between devices: 219 us -> none  [local(): spectra = lax.psum(partial_terms, 'lat')]
    psum x1 -> x0, blocking collectives: 134 us -> none  [local(): grad_weight = lax.psum(weight_part, 'lon')]
    all_to_all x1 -> x3, waiting for transfers between devices: 0.01 us -> 44.9 us  [the longest x1 24.3 us: local(): got = lax.all_to_all(sent, ('z',), 0, 0, tiled=True)]
    all_to_all x1 -> x3, starting transfers between devices: 8.65 us -> 27.6 us  [the longest x1 17 us: local(): lax.all_to_all(coeffs.reshape(128, 4, 128), GROUP, 0, 0, tiled=True)]
    all_to_all x1 -> x2, blocking collectives: 18.9 us -> 35.6 us  [the longest x1 29.6 us: local(): back = lax.all_to_all(back, GROUP, 0, 0, tiled=True)]
    ppermute x0 -> x2, starting transfers between devices: none -> 11.9 us  [the longest x1 9.76 us: local(): lax.ppermute(other, ('yh', 'xl', 'c'), [(a * 4 + x * 2 + b, b * 4 + (1 -...]
    reshape x3 -> x11, local copies, waits for them, and re-layouts: 2.05 us -> 9.24 us  [the longest x1 2.49 us: local(): sv = got[..., degrees:].reshape(degrees, 2, 2, quarter)]
    slice x1 -> x9, local copies, waits for them, and re-layouts: 0.22 us -> 7.14 us  [the longest x1 4.06 us: local(): sv = jnp.where(c == 0, sv[:, :, 0], sv[:, :, 1]).transpose(1, 2, 0)]
  transfers between devices with their start and end apart: 2 -> 5, of which waited for: 1 -> 4; matrix products, arithmetic and copies ran while one was open for 1% -> 9% of each run, Pallas kernels for 0% -> 0%
where the time goes in v1:
time: 170 us; the launch traced here: 169 us
  waiting for transfers between devices  46.7 us (27%)
  starting transfers between devices  39.6 us (23%)
  blocking collectives  35.6 us (21%)
  local copies, waits for them, and re-layouts  31.2 us (18%)
  matrix products  7.98 us (5%)
  other arithmetic  6.92 us (4%)
    all_to_all x1, blocking collectives, local(): back = lax.all_to_all(back, GROUP, 0, 0, tiled=True)  29.6 us
    all_to_all x1, waiting for transfers between devices, local(): got = lax.all_to_all(sent, ('z',), 0, 0, tiled=True)  24.3 us
    all_to_all x1, starting transfers between devices, local(): lax.all_to_all(coeffs.reshape(128, 4, 128), GROUP, 0, 0, tiled=True)  17 us
    all_to_all x1, waiting for transfers between devices, local(): lax.all_to_all(coeffs.reshape(128, 4, 128), GROUP, 0, 0, tiled=True)  14.9 us
    ppermute x1, starting transfers between devices, local(): lax.ppermute(other, ('yh', 'xl', 'c'), [(a * 4 + x * 2 + b, b * 4 + (1 -...  9.76 us
    unnamed x32, local copies, waits for them, and re-layouts  8.53 us
    all_to_all x1, starting transfers between devices, local(): lax.all_to_all(jnp.broadcast_to(share, (32, 4, 128)), LON, 0, 0, tiled=True)  6.15 us
    all_to_all x1, blocking collectives, local(): got = lax.all_to_all(jnp.stack([got, got]), ('c',), 0, 0, tiled=True)  6 us
  transfers between devices with their start and end apart: 5, of which 4 were waited for; matrix products, arithmetic and copies ran while one was open for 9% of the time, Pallas kernels for 0%

profile of v1, /device:TPU:1, one launch (start us, length us, event | category | flops | bytes accessed | tf_op | source)
XLA Modules:
  0.0 169.1 jit_solution(2865732296125837278)
XLA Ops:
  0.6 1.1 reshape.106
  1.8 1.8 %convolution_bitcast_fusion.2 = f32[270,160]{0,1:T(8,128)S(1)} fusion(f32[270,160]{1,0:T(8,128)S(1)} %reshape.106, f32[2,160,160]{2,1,0:T(8,128)} %constant.40.clone, s32[]{:T(128)S(6)} %select_n.27), kind=kOutput, calls=%fused_computation.12 | convolution fusion | flops 82944000 | bytes 509444 | tf_op jit(solution)/shard_map/dot_general | solution.py:62
  4.6 0.9 pad_maximum_fusion.2
  5.5 9.8 %collective-permute-start.1 = (f32[3,45,880]{2,1,0:T(8,128)S(1)}, f32[3,45,880]{2,1,0:T(8,128)}, u32[]{:S(2)}, u32[]{:S(2)}) collective-permute-start(f32[3,45,880]{2,1,0:T(8,128)S(1)} %get-tuple-element.24), channel_id=1, source_target_pairs={{0,2},{1,258},{2,0},{3,256},{256,3},{257,259},{258,1},{259,257},{4... | collective-permute-start | bytes 1425608 | tf_op jit(solution)/shard_map/ppermute | solution.py:67
  15.3 2.2 %collective-permute-start = (f32[3,45,880]{2,1,0:T(8,128)}, f32[3,45,880]{2,1,0:T(8,128)S(1)}, u32[]{:S(2)}, u32[]{:S(2)}) collective-permute-start(f32[3,45,880]{2,1,0:T(8,128)} %get-tuple-element.25), channel_id=1, source_target_pairs={{0,0},{1,256},{256,1},{257,257},{2,2},{3,258},{258,3},{259,259},{4... | collective-permute-start | bytes 1425608 | tf_op jit(solution)/shard_map/ppermute | solution.py:66
  17.6 0.8 fusion.2
  18.5 0.8 copy.94
  19.3 17.0 %all-to-all-start = ((f32[128,4,128]{2,1,0:T(4,128)}), f32[128,4,128]{2,1,0:T(4,128)S(1)}, u32[]{:S(2)}, u32[]{:S(2)}) async-start(f32[128,4,128]{2,1,0:T(4,128)} %copy.94), calls=%async_computation | async-start | bytes 524288 | tf_op jit(solution)/shard_map/all_to_all | solution.py:77
  36.3 1.8 %collective-permute-done = f32[3,45,880]{2,1,0:T(8,128)S(1)} collective-permute-done((f32[3,45,880]{2,1,0:T(8,128)}, f32[3,45,880]{2,1,0:T(8,128)S(1)}, u32[]{:S(2)}, u32[]{:S(2)}) %collective-permute-start) | collective-permute-done | bytes 475232 | tf_op jit(solution)/shard_map/ppermute | solution.py:66
  38.1 2.2 %pad_maximum_fusion.1 = f32[8,45,880]{2,1,0:T(8,128)} fusion(f32[2,45,880]{2,1,0:T(8,128)S(1)} %slice.110, f32[3,45,880]{2,1,0:T(8,128)} %collective-permute-done.1, f32[3,45,880]{2,1,0:T(8,128)S(1)} %collective-permute-done), kind=kLoop, calls=%fused_computation.9 | loop fusion | flops 633600 | bytes 2534400 | tf_op jit(solution)/shard_map/concatenate | solution.py:79
  40.3 14.9 %all-to-all-done = f32[128,4,128]{2,1,0:T(4,128)S(1)} async-done(((f32[128,4,128]{2,1,0:T(4,128)}), f32[128,4,128]{2,1,0:T(4,128)S(1)}, u32[]{:S(2)}, u32[]{:S(2)}) %all-to-all-start) | async-done | bytes 262176 | tf_op jit(solution)/shard_map/all_to_all | solution.py:77
  55.3 4.5 %all-to-all-start.1 = ((f32[8,45,880]{2,1,0:T(8,128)}), f32[8,45,880]{2,1,0:T(8,128)}, u32[]{:S(2)}, u32[]{:S(2)}) async-start(f32[8,45,880]{2,1,0:T(8,128)} %pad_maximum_fusion.1), calls=%async_computation.1 | async-start | bytes 2752512 | tf_op jit(solution)/shard_map/all_to_all | solution.py:81
  59.8 1.1 copy.87
  60.9 1.0 reshape.104
  62.0 1.4 convolution_bitcast_fusion.1
  63.4 0.3 copy.88
  63.7 0.8 reshape.105
  64.5 1.1 fusion.18
  65.7 0.8 copy.119
  66.5 1.5 copy.118
  68.0 0.4 reshape.112
  68.4 0.4 copy.95
  68.8 1.0 reshape.113
  69.8 24.3 %all-to-all-done.1 = f32[8,45,880]{2,1,0:T(8,128)} async-done(((f32[8,45,880]{2,1,0:T(8,128)}), f32[8,45,880]{2,1,0:T(8,128)}, u32[]{:S(2)}, u32[]{:S(2)}) %all-to-all-start.1) | async-done | bytes 1267232 | tf_op jit(solution)/shard_map/all_to_all | solution.py:81
  94.1 2.0 %pad_maximum_fusion = f32[2,8,45,880]{3,2,1,0:T(8,128)S(1)} fusion(f32[1,8,45,880]{3,2,1,0:T(8,128)} %bitcast.13), kind=kLoop, calls=%fused_computation | loop fusion | flops 633600 | bytes 3801600 | tf_op jit(solution)/shard_map/stack | solution.py:82
  96.1 0.8 copy.96
  96.9 6.0 %all_to_all.25 = f32[2,8,45,880]{3,1,2,0:T(8,128)S(1)} all-to-all(f32[2,8,45,880]{3,1,2,0:T(8,128)S(1)} %copy.96), channel_id=1, replica_groups=mesh['yh'=2,'z'=8,'yl'=4,'xh'=2,'xl'=2,'c'=2] {'c'}, dimensions={0} | all-to-all | bytes 5068800 | tf_op jit(solution)/shard_map/all_to_all | solution.py:82
  102.9 0.5 copy.97
  103.4 0.3 slice.116
  103.9 2.5 %reshape.131 = f32[720,2,2,40]{3,2,1,0:T(2,128)} reshape(f32[16,45,160]{2,1,0:T(8,128)S(1)} %slice.116) | data formatting | bytes 921600 | tf_op jit(solution)/shard_map/reshape | solution.py:85
  106.4 4.1 %fusion.19 = (f32[720,2,1,40]{3,2,1,0:T(1,128)}, f32[720,2,1,40]{3,2,1,0:T(1,128)S(1)}) fusion(f32[720,2,2,40]{3,2,1,0:T(2,128)} %reshape.131), kind=kLoop, calls=%fused_computation.43 | loop fusion | bytes 921600 | tf_op jit(solution)/shard_map/slice | solution.py:86
  110.5 1.9 %copy.121 = f32[720,2,1,40]{0,3,1,2:T(8,128)} copy(f32[720,2,1,40]{3,2,1,0:T(1,128)} %get-tuple-element.16) | data formatting | bytes 460800
  112.4 1.5 copy.120
  114.1 0.7 copy-done.7
  114.8 0.9 fusion.22
  116.2 0.2 stack.37
  117.0 2.2 %fusion.3 = f32[1,2,8,5,16,48]{5,2,4,3,1,0:T(8,128)S(1)} fusion(f32[1,8,5,720]{3,1,2,0:T(8,128)S(1)} %copy.100, f32[1,8,5,720]{3,1,2,0:T(8,128)S(1)} %copy.99, f32[]{:T(128)S(6)} %select_n.30, f32[16,45,720]{2,1,0:T(8,128)S(1)} %slice.112), kind=kOutput, calls=%fused_computation.11 | convolution fusion | flops 265536000 | bytes 2549764 | tf_op jit(solution)/shard_map/rhl,pl->rhp/dot_general | solution.py:105
  119.4 0.8 copy.106
  120.2 1.2 reshape.117
  121.5 29.6 %all_to_all.26 = f32[128,8,128]{2,1,0:T(8,128)S(1)} all-to-all(f32[128,8,128]{2,1,0:T(8,128)S(1)} %bitcast.95), channel_id=1, replica_groups=mesh['yh'=2,'z'=8,'yl'=4,'xh'=2,'xl'=2,'c'=2] {'yh','z','yl','xh'}, dimensions={0} | all-to-all | bytes 1048576 | tf_op jit(solution)/shard_map/all_to_all | solution.py:111
  151.1 1.0 copy.107
  152.1 1.1 slice.121
  153.5 0.6 broadcast_in_dim.9
  154.1 6.1 %all-to-all-start.4 = ((f32[32,4,128]{2,1,0:T(4,128)}), f32[32,4,128]{2,1,0:T(4,128)S(1)}, u32[]{:S(2)}, u32[]{:S(2)}) async-start(f32[32,4,128]{2,1,0:T(4,128)} %broadcast_in_dim.9), calls=%async_computation.4 | async-start | bytes 131072 | tf_op jit(solution)/shard_map/all_to_all | solution.py:116
  160.3 0.8 convolution_bitcast_fusion
  161.1 1.3 slice_multiply_fusion
  162.5 5.7 %all-to-all-done.4 = f32[32,4,128]{2,1,0:T(4,128)S(1)} async-done(((f32[32,4,128]{2,1,0:T(4,128)}), f32[32,4,128]{2,1,0:T(4,128)S(1)}, u32[]{:S(2)}, u32[]{:S(2)}) %all-to-all-start.4) | async-done | bytes 65568 | tf_op jit(solution)/shard_map/all_to_all | solution.py:116
  168.4 0.8 copy.109
  (56 shorter events, 3.3 us)
Async XLA Ops:
  3.6 1.0 copy-start.8
  4.2 13.3 %copy-start.2 = (f32[5,45,1440]{2,1,0:T(8,128)S(1)}, f32[5,45,1440]{2,1,0:T(8,128)}, u32[]{:S(2)}) copy-start(f32[5,45,1440]{2,1,0:T(8,128)} %param.7) | copy-start | bytes 3888004
  5.5 32.6 %collective-permute-start.1 = (f32[3,45,880]{2,1,0:T(8,128)S(1)}, f32[3,45,880]{2,1,0:T(8,128)}, u32[]{:S(2)}, u32[]{:S(2)}) collective-permute-start(f32[3,45,880]{2,1,0:T(8,128)S(1)} %get-tuple-element.24), channel_id=1, source_target_pairs={{0,2},{1,258},{2,0},{3,256},{256,3},{257,259},{258,1},{259,257},{4... | collective-permute-start | bytes 1425608 | tf_op jit(solution)/shard_map/ppermute | solution.py:67
  15.3 2.4 %copy-start = (f32[2,2,128,1440]{2,3,1,0:T(8,128)S(1)}, f32[2,2,128,1440]{2,3,1,0:T(8,128)}, u32[]{:S(2)}) copy-start(f32[2,2,128,1440]{2,3,1,0:T(8,128)} %constant.41.clone) | copy-start | bytes 8847364
  15.3 22.8 %collective-permute-start = (f32[3,45,880]{2,1,0:T(8,128)}, f32[3,45,880]{2,1,0:T(8,128)S(1)}, u32[]{:S(2)}, u32[]{:S(2)}) collective-permute-start(f32[3,45,880]{2,1,0:T(8,128)} %get-tuple-element.25), channel_id=1, source_target_pairs={{0,0},{1,256},{256,1},{257,257},{2,2},{3,258},{258,3},{259,259},{4... | collective-permute-start | bytes 1425608 | tf_op jit(solution)/shard_map/ppermute | solution.py:66
  19.3 36.0 %all-to-all-start = ((f32[128,4,128]{2,1,0:T(4,128)}), f32[128,4,128]{2,1,0:T(4,128)S(1)}, u32[]{:S(2)}, u32[]{:S(2)}) async-start(f32[128,4,128]{2,1,0:T(4,128)} %copy.94), calls=%async_computation | async-start | bytes 524288 | tf_op jit(solution)/shard_map/all_to_all | solution.py:77
  40.3 19.4 %copy-start.3 = (f32[720,2,160]{0,2,1:T(8,128)S(1)}, f32[720,2,160]{0,2,1:T(8,128)}, u32[]{:S(2)}) copy-start(f32[720,2,160]{0,2,1:T(8,128)} %param.9) | copy-start | bytes 2764804
  55.3 38.8 %all-to-all-start.1 = ((f32[8,45,880]{2,1,0:T(8,128)}), f32[8,45,880]{2,1,0:T(8,128)}, u32[]{:S(2)}, u32[]{:S(2)}) async-start(f32[8,45,880]{2,1,0:T(8,128)} %pad_maximum_fusion.1), calls=%async_computation.1 | async-start | bytes 2752512 | tf_op jit(solution)/shard_map/all_to_all | solution.py:81
  60.9 1.0 copy-start.9
  113.9 0.9 copy-start.7
  114.0 1.7 %copy-start.4 = (f32[720,2,1,40]{0,3,1,2:T(8,128)S(1)}, f32[720,2,1,40]{0,3,1,2:T(8,128)}, u32[]{:S(2)}) copy-start(f32[720,2,1,40]{0,3,1,2:T(8,128)} %copy.118) | copy-start | bytes 691204
  114.1 1.7 %copy-start.5 = (f32[720,2,1,40]{0,3,1,2:T(8,128)S(1)}, f32[720,2,1,40]{0,3,1,2:T(8,128)}, u32[]{:S(2)}) copy-start(f32[720,2,1,40]{0,3,1,2:T(8,128)} %copy.121) | copy-start | bytes 691204
  114.1 1.7 %copy-start.6 = (f32[720,2,1,40]{0,3,1,2:T(8,128)S(1)}, f32[720,2,1,40]{0,3,1,2:T(8,128)}, u32[]{:S(2)}) copy-start(f32[720,2,1,40]{0,3,1,2:T(8,128)} %copy.120) | copy-start | bytes 691204
  151.1 9.2 %copy-start.1 = (f32[2,2,128,1440]{2,3,1,0:T(8,128)S(1)}, f32[2,2,128,1440]{2,3,1,0:T(8,128)}, u32[]{:S(2)}) copy-start(f32[2,2,128,1440]{2,3,1,0:T(8,128)} %constant.41.clone) | copy-start | bytes 8847364
  154.1 14.0 %all-to-all-start.4 = ((f32[32,4,128]{2,1,0:T(4,128)}), f32[32,4,128]{2,1,0:T(4,128)S(1)}, u32[]{:S(2)}, u32[]{:S(2)}) async-start(f32[32,4,128]{2,1,0:T(4,128)} %broadcast_in_dim.9), calls=%async_computation.4 | async-start | bytes 131072 | tf_op jit(solution)/shard_map/all_to_all | solution.py:116
  160.3 0.8 copy-start.10

commit v2 on v1

v2 whole, which is shorter than its diff:
```python
import functools
import math

import jax
import jax.numpy as jnp
import ml_dtypes
import numpy as np
from jax import lax
from jax.experimental import pallas as pl
from jax.experimental.pallas import tpu as pltpu
from jax.sharding import Mesh, PartitionSpec as P

NAMES = ("yh", "z", "yl", "xh", "xl", "c")
SIZES = (2, 8, 4, 2, 2, 2)
LAT = ("yh", "z")
LON = ("yl", "xh", "xl", "c")
GROUP = ("yh", "z", "yl", "xh")
BF = jnp.bfloat16
F32 = jnp.float32
WIDE = 48
NN = (((1,), (0,)), ((), ()))
NT = (((1,), (1,)), ((), ()))
TN = (((0,), (0,)), ((), ()))


def order_of(yh, z, yl, xh, xl):
    xl_o = np.where(z < 3, xl, 1 - xl)
    m = 3 * (((yl * 2 + xh) * 2 + xl_o) * 2 + yh) + z % 3
    return np.where(z < 6, m, -1)


@functools.cache
def tables(points):
    yh, z, yl, xh = np.meshgrid(*[np.arange(n) for n in SIZES[:4]], indexing="ij")
    out = []
    for xl in range(2):
        m = order_of(yh, z, yl, xh, xl).reshape(-1)
        phase = (m[:, None] * np.arange(points)[None]) % points
        angle = 2.0 * math.pi / points * phase
        rows = np.stack([np.cos(angle), -np.sin(angle)]) / math.sqrt(points)
        out.append(np.where(m[None, :, None] >= 0, rows, 0.0).reshape(256, points))
    full = np.stack(out).astype(np.float32)
    high = full.astype(ml_dtypes.bfloat16)
    low = (full - high.astype(np.float32)).astype(ml_dtypes.bfloat16)
    return high, low


@functools.cache
def channel_slots(channels):
    per = channels // 32
    out = []
    for xl in range(2):
        out.append(
            [
                (((yl * 2 + xh) * 2 + region) * 2 + c) * per + j
                for region in (xl, 1 - xl)
                for c in range(2)
                for j in range(per)
                for yl in range(4)
                for xh in range(2)
            ]
        )
    return np.asarray(out, np.int32)


def dot(a, b, dims):
    return lax.dot_general(a, b, dims, preferred_element_type=F32)


def two(x):
    high = x.astype(BF)
    return high, (x - high.astype(F32)).astype(BF)


def three(x):
    high, rest = x.astype(BF), None
    rest = x - high.astype(F32)
    mid = rest.astype(BF)
    return high, mid, (rest - mid.astype(F32)).astype(BF)


def params(flops, nbytes, vmem=48):
    return dict(
        compiler_params=pltpu.CompilerParams(vmem_limit_bytes=vmem * 2**20),
        cost_estimate=pl.CostEstimate(flops=flops, bytes_accessed=nbytes, transcendentals=0),
    )


def prepare_kernel(slots_ref, leg_ref, saved_ref, own_ref, other_ref):
    orders, rows, degrees = leg_ref.shape
    channels = saved_ref.shape[3]
    half = channels // 2
    pick = (lax.broadcasted_iota(jnp.int32, (channels, channels), 0) == slots_ref[...]).astype(F32).astype(BF)
    for k in range(orders):
        for ref in (own_ref, other_ref):
            ref[k, WIDE - 8 : WIDE, :] = jnp.zeros((8, ref.shape[2]), F32)
            ref[k, :rows, :degrees] = leg_ref[k]
            ref[k, :, degrees + channels :] = jnp.zeros((WIDE, ref.shape[2] - degrees - channels), F32)
        for r in range(2):
            v = saved_ref[:, k, r, :]
            out = sum(dot(term, pick, NN) for term in three(v))
            at = degrees + r * half
            own_ref[k, :rows, at : at + half] = out[:, :half]
            other_ref[k, :rows, at : at + half] = out[:, half:]


def weight_kernel(place_ref, slots_ref, w_ref, out_ref):
    degrees, _, channels = w_ref.shape
    quarter = channels // 4
    pick = (lax.broadcasted_iota(jnp.int32, (channels, 2 * quarter), 0) == slots_ref[...]).astype(F32).astype(BF)
    c = place_ref[1]
    for r in range(2):
        out = sum(dot(pick, term, (((0,), (1,)), ((), ()))) for term in three(w_ref[:, r, :]))
        out_ref[r * quarter : (r + 1) * quarter, :] = jnp.where(
            c == 0, out[:quarter], out[quarter : 2 * quarter]
        )


def forward_kernel(place_ref, g_ref, th_ref, tl_ref, out_ref, field):
    group, rows, points = g_ref.shape
    field[...] = jnp.zeros_like(field)
    for j in range(group):
        field[j * WIDE : j * WIDE + rows, :] = g_ref[j]
    high, low = two(field[...])
    table = th_ref[0]
    acc = dot(table, high, NT) + dot(table, low, NT) + dot(tl_ref[0], high, NT)
    for r in range(2):
        for k in range(2):
            out_ref[:, 2 * r + k, :] = acc[r * 128 : (r + 1) * 128, k * 128 : (k + 1) * 128]


def split_kernel(place_ref, near_ref, far_ref, lh_ref, ll_ref, sv_ref, dense):
    blocks, _, _ = near_ref.shape
    degrees = lh_ref.shape[1]
    span = blocks * WIDE
    quarter = sv_ref.shape[0] // 2
    c = place_ref[1]
    for ref, side in ((near_ref, c), (far_ref, 1 - c)):
        at = pl.multiple_of(side * span, span)
        x = ref[...].reshape(span, ref.shape[2])
        high, low = two(x[:, :degrees])
        lh_ref[pl.ds(at, span), :] = high
        ll_ref[pl.ds(at, span), :] = low
        dense[pl.ds(at, span), :] = x[:, degrees - degrees % 128 :]
    turned = dense[...].T
    off = degrees % 128
    for r in range(2):
        first = turned[off + (2 * r) * quarter : off + (2 * r + 1) * quarter]
        second = turned[off + (2 * r + 1) * quarter : off + (2 * r + 2) * quarter]
        mine = jnp.where(c == 0, first, second)
        for a in range(2 * blocks):
            sv_ref[r * quarter : (r + 1) * quarter, a * 45 : a * 45 + 45] = mine[:, a * WIDE : a * WIDE + 45]


def core_kernel(place_ref, x_ref, lh_ref, ll_ref, sv_ref, w_ref, out_ref, ct, tmp, back):
    group, bands = 5, 16
    quarter = sv_ref.shape[0] // 2
    rows = 45
    back[...] = jnp.zeros_like(back)
    for k in range(4):
        tmp[:, k * 128 : (k + 1) * 128] = x_ref[:, k, :]
    for a in range(bands):
        for r in range(2):
            for j in range(group):
                q = (r * group + j) * 8
                lane = r * 256 + j * WIDE
                ct[q : q + 8, a * WIDE : (a + 1) * WIDE] = tmp[a * 8 : a * 8 + 8, lane : lane + WIDE]
    ch, cl = two(ct[...])
    n = 2 * quarter
    both = dot(jnp.concatenate([ch, cl], axis=0), lh_ref[...], NN)
    spec = both[:n] + both[n:] + dot(ch, ll_ref[...], NN)
    g, h = spec[:quarter], spec[quarter:]
    u, v = w_ref[:quarter, :], w_ref[quarter:, :]
    twice = jnp.where(place_ref[2] == 1, 1.0, 2.0).astype(F32)
    adjoint = jnp.concatenate([(u * g + v * h) * twice, (u * h - v * g) * twice], axis=0)
    p, q = sv_ref[:quarter, :], sv_ref[quarter:, :]
    part = (p * g + q * h, p * h - q * g)
    ah, al = two(adjoint)
    both = dot(jnp.concatenate([ah, al], axis=0), lh_ref[...], NT)
    syn = both[:n] + both[n:] + dot(ah, ll_ref[...], NT)
    for a in range(bands):
        for r in range(2):
            for j in range(group):
                at = (r * group + j) * 8
                lane = r * 256 + j * WIDE
                back[a * 8 : a * 8 + 8, lane : lane + WIDE] = syn[at : at + 8, a * WIDE : (a + 1) * WIDE]
                back[a * 8 : a * 8 + 8, 512 + lane : 512 + lane + rows] = part[r][
                    j * 8 : j * 8 + 8, a * rows : (a + 1) * rows
                ]
    for k in range(8):
        out_ref[:, k, :] = back[:, k * 128 : (k + 1) * 128]


def share_kernel(x_ref, out_ref):
    total = jnp.sum(x_ref[...], axis=0)[4:8]
    out_ref[...] = jnp.broadcast_to(total[None], out_ref.shape)


def inverse_kernel(place_ref, x_ref, th_ref, tl_ref, lw_ref, out_ref):
    group, rows, points = out_ref.shape
    block = jnp.concatenate(
        [jnp.concatenate([x_ref[:, 2 * r, :], x_ref[:, 2 * r + 1, :]], axis=1) for r in range(2)], axis=0
    )
    high, low = two(block)
    table = th_ref[0]
    acc = dot(high, table, TN) + dot(low, table, TN) + dot(high, tl_ref[0], TN)
    for j in range(group):
        out_ref[j] = acc[j * WIDE : j * WIDE + rows] * lw_ref[...]


def whole(shape):
    return pl.BlockSpec(shape, lambda i, place: (0,) * len(shape))


def call(kernel, place, args, out_shapes, scratch=(), picked=(), **extra):
    specs = []
    for i, a in enumerate(args):
        if i in picked:
            specs.append(pl.BlockSpec((1, *a.shape[1:]), lambda _, p, n=a.ndim: (p[0],) + (0,) * (n - 1)))
        else:
            specs.append(whole(a.shape))
    return pl.pallas_call(
        kernel,
        out_shape=out_shapes,
        grid_spec=pltpu.PrefetchScalarGridSpec(
            num_scalar_prefetch=1,
            grid=(1,),
            in_specs=specs,
            out_specs=jax.tree.map(lambda s: whole(s.shape), out_shapes),
            scratch_shapes=list(scratch),
        ),
        **extra,
    )(place, *args)


def drop_place(kernel):
    return lambda place_ref, *refs: kernel(*refs)


def shape(*dims, dtype=F32):
    return jax.ShapeDtypeStruct(dims, dtype)


def local(grad_out, saved_spectra, spec_weight, legendre, lat_weight):
    group, rows, points = grad_out.shape
    degrees, _, channels = spec_weight.shape
    orders = legendre.shape[0]
    lanes = -(-(degrees + channels) // 128) * 128
    half, quarter = channels // 2, channels // 4
    yh, z, yl, xh, xl, c = (lax.axis_index(n) for n in NAMES)
    first = (yl + xh + yh == 0) & (z == 3 * xl)
    place = jnp.stack([xl, c, first.astype(jnp.int32)]).astype(jnp.int32)
    slot_table = jnp.asarray(channel_slots(channels))
    slots = jnp.where(xl == 0, slot_table[0:1], slot_table[1:2])
    high, low = (jnp.asarray(t) for t in tables(points))

    own, other = call(
        drop_place(prepare_kernel),
        place,
        (slots, legendre, saved_spectra),
        (shape(orders, WIDE, lanes), shape(orders, WIDE, lanes)),
        **params(60_000_000, 4_000_000),
    )
    own = lax.ppermute(own, ("yh", "c"), [(a * 2 + b, b * 2 + a) for a in range(2) for b in range(2)])
    other = lax.ppermute(
        other,
        ("yh", "xl", "c"),
        [(a * 4 + x * 2 + b, b * 4 + (1 - x) * 2 + a) for a in range(2) for x in range(2) for b in range(2)],
    )
    sent = jnp.concatenate([own, other, own[:2]], axis=0)
    near = lax.all_to_all(sent, ("z",), 0, 0, tiled=True)
    far = lax.ppermute(near, ("c",), [(0, 1), (1, 0)])

    coeffs = call(
        forward_kernel,
        place,
        (grad_out, high, low),
        shape(128, 4, 128),
        scratch=[pltpu.VMEM((256, points), F32)],
        picked=(1, 2),
        **params(600_000_000, 3_000_000),
    )
    weight = call(
        weight_kernel, place, (slots[:, :half], spec_weight), shape(2 * quarter, degrees),
        **params(200_000_000, 2_000_000),
    )
    coeffs, near_done = lax.optimization_barrier((coeffs, near))
    coeffs = lax.all_to_all(coeffs, GROUP, 0, 0, tiled=True)
    leg_high, leg_low, sv = call(
        split_kernel,
        place,
        (near_done, far),
        (
            shape(16 * WIDE, degrees, dtype=BF),
            shape(16 * WIDE, degrees, dtype=BF),
            shape(2 * quarter, degrees),
        ),
        scratch=[pltpu.VMEM((16 * WIDE, lanes - degrees + degrees % 128), F32)],
        **params(100_000_000, 6_000_000),
    )
    back = call(
        core_kernel,
        place,
        (coeffs, leg_high, leg_low, sv, weight),
        shape(128, 8, 128),
        scratch=[
            pltpu.VMEM((2 * quarter, 16 * WIDE), F32),
            pltpu.VMEM((128, 512), F32),
            pltpu.VMEM((128, 1024), F32),
        ],
        **params(600_000_000, 4_000_000),
    )
    back = lax.all_to_all(back, GROUP, 0, 0, tiled=True)

    share = call(drop_place(share_kernel), place, (back,), shape(32, 4, 128), **params(1_000_000, 700_000))
    share = lax.all_to_all(share, LON, 0, 0, tiled=True)
    grad_in = call(
        inverse_kernel,
        place,
        (back, high, low, lat_weight.reshape(rows, 1)),
        shape(group, rows, points),
        picked=(1, 2),
        **params(600_000_000, 4_000_000),
    )
    grad_weight = share.reshape(32, 512)[:, :].reshape(32, 2, 256)[..., : group * WIDE]
    grad_weight = grad_weight.reshape(32, 2, group, WIDE)[..., :rows]
    grad_weight = grad_weight.transpose(3, 1, 0, 2).reshape(rows, 2, channels)
    return (grad_in, grad_weight)


def solution(mesh):
    fine = Mesh(mesh.devices.reshape(SIZES), NAMES)
    return jax.shard_map(
        local,
        mesh=fine,
        in_specs=(P(LON, LAT, None), P(LAT, LON, None, None), P(), P(LON, LAT, None), P(LAT)),
        out_specs=(P(LON, LAT, None), P(LAT, None, None)),
        check_vma=False,
    )
```

time: 170 us -> 169 us (level)
  blocking collectives: 35.6 us -> 66.3 us
  Pallas kernels: 0 us -> 25.2 us
  waiting for transfers between devices: 46.7 us -> 23.5 us
  local copies, waits for them, and re-layouts: 31.2 us -> 17.6 us
  matrix products: 7.98 us -> 0 us
  other arithmetic: 6.92 us -> 0.86 us
  starting transfers between devices: 39.6 us -> 33.8 us
    all_to_all x3 -> x2, waiting for transfers between devices: 44.9 us -> 4.13 us  [the longest x1 4.13 us: local(): share = lax.all_to_all(share, LON, 0, 0, tiled=True)]
    all_to_all x1, blocking collectives: 6 us -> 31.5 us  [local(): near = lax.all_to_all(sent, ('z',), 0, 0, tiled=True)]
    pallas_call x0 -> x7, Pallas kernels: none -> 25.2 us  [call(): pl.pallas_call(kernel, out_shape=out_shapes, grid_spec=pltpu.PrefetchScal...]
    ppermute x1, waiting for transfers between devices: 0.01 us -> 13.6 us  [local(): lax.ppermute(other, ('yh', 'xl', 'c'), [(a * 4 + x * 2 + b, b * 4 + (1 -...]
    reshape x11 -> x2, local copies, waits for them, and re-layouts: 9.24 us -> 0.21 us  [the longest x1 0.1 us: local(): lat_weight.reshape(rows, 1)]
    unnamed x32 -> x37, local copies, waits for them, and re-layouts: 8.53 us -> 17.2 us
    dot_general x6 -> x0, matrix products: 7.98 us -> none  [the longest x1 2.23 us: local(): synthesis = jnp.einsum('rhl,pl->rhp', adjoint, leg, precision=HIGH)]
    all_to_all x3 -> x2, starting transfers between devices: 27.6 us -> 20.2 us  [the longest x1 13.6 us: local(): coeffs = lax.all_to_all(coeffs, GROUP, 0, 0, tiled=True)]
  transfers between devices with their start and end apart: 5 -> 5, of which waited for: 4 -> 3; matrix products, arithmetic and copies ran while one was open for 9% -> 2% of each run, Pallas kernels for 0% -> 11%
where the time goes in v2:
time: 169 us; the launch traced here: 168 us
  blocking collectives  66.3 us (39%)
  starting transfers between devices  33.8 us (20%)
  Pallas kernels  25.2 us (15%)
  waiting for transfers between devices  23.5 us (14%)
  local copies, waits for them, and re-layouts  17.6 us (10%)
    all_to_all x1, blocking collectives, local(): back = lax.all_to_all(back, GROUP, 0, 0, tiled=True)  34.8 us
    all_to_all x1, blocking collectives, local(): near = lax.all_to_all(sent, ('z',), 0, 0, tiled=True)  31.5 us
    pallas_call x7, Pallas kernels, call(): pl.pallas_call(kernel, out_shape=out_shapes, grid_spec=pltpu.PrefetchScal...  25.2 us
    unnamed x37, local copies, waits for them, and re-layouts  17.2 us
    all_to_all x1, starting transfers between devices, local(): coeffs = lax.all_to_all(coeffs, GROUP, 0, 0, tiled=True)  13.6 us
    ppermute x1, waiting for transfers between devices, local(): lax.ppermute(other, ('yh', 'xl', 'c'), [(a * 4 + x * 2 + b, b * 4 + (1 -...  13.6 us
    ppermute x1, starting transfers between devices, local(): lax.ppermute(own, ('yh', 'c'), [(a * 2 + b, b * 2 + a) for a in range(2)...  8.85 us
    all_to_all x1, starting transfers between devices, local(): share = lax.all_to_all(share, LON, 0, 0, tiled=True)  6.53 us
  transfers between devices with their start and end apart: 5, of which 3 were waited for; matrix products, arithmetic and copies ran while one was open for 2% of the time, Pallas kernels for 11%

profile of v2, /device:TPU:1, one launch (start us, length us, event | category | flops | bytes accessed | tf_op | source)
XLA Modules:
  0.0 168.0 jit_solution(5672131124022736099)
XLA Ops:
  0.6 0.1 pad_add_fusion.place_ref
  0.7 0.7 broadcast_select_fusion.refs_0_
  1.4 1.0 copy-done.12
  2.4 1.0 copy-done.13
  3.4 2.3 %shard_map.96 = (f32[3,48,896]{2,1,0:T(8,128)S(1)}, f32[3,48,896]{2,1,0:T(8,128)S(1)}) custom-call(s32[3]{0:T(128)S(1)} %pad_add_fusion.place_ref, s32[1,160]{1,0:T(1,128)S(1)} %broadcast_select_fusion.refs_0_, f32[3,45,720]{2,1,0:T(8,128)S(1)} %copy-done.12, f32[45,3,2,160]{3,2,1,0:T(2,128)S(1)} %copy-done.13), custom_call_target="tpu_custom_call" | custom-call | flops 60000000 | bytes 4000000 | tf_op jit(solution)/shard_map/pallas_call | solution.py:222
  5.7 8.8 %collective-permute-start = (f32[3,48,896]{2,1,0:T(8,128)S(1)}, f32[3,48,896]{2,1,0:T(8,128)S(1)}, u32[]{:S(2)}, u32[]{:S(2)}) collective-permute-start(f32[3,48,896]{2,1,0:T(8,128)S(1)} %get-tuple-element.9), channel_id=1, source_target_pairs={{0,0},{1,256},{256,1},{257,257},{2,2},{3,258},{258,3},{259,259},{4... | collective-permute-start | bytes 1548296 | tf_op jit(solution)/shard_map/ppermute | solution.py:264
  14.5 2.8 %collective-permute-start.1 = (f32[3,48,896]{2,1,0:T(8,128)S(1)}, f32[3,48,896]{2,1,0:T(8,128)S(1)}, u32[]{:S(2)}, u32[]{:S(2)}) collective-permute-start(f32[3,48,896]{2,1,0:T(8,128)S(1)} %get-tuple-element.10), channel_id=1, source_target_pairs={{0,2},{1,258},{2,0},{3,256},{256,3},{257,259},{258,1},{259,257},{4... | collective-permute-start | bytes 1548296 | tf_op jit(solution)/shard_map/ppermute | solution.py:265
  17.4 5.8 %collective-permute-done = f32[3,48,896]{2,1,0:T(8,128)S(1)} collective-permute-done((f32[3,48,896]{2,1,0:T(8,128)S(1)}, f32[3,48,896]{2,1,0:T(8,128)S(1)}, u32[]{:S(2)}, u32[]{:S(2)}) %collective-permute-start) | collective-permute-done | bytes 516128 | tf_op jit(solution)/shard_map/ppermute | solution.py:264
  23.2 13.6 %collective-permute-done.1 = f32[3,48,896]{2,1,0:T(8,128)S(1)} collective-permute-done((f32[3,48,896]{2,1,0:T(8,128)S(1)}, f32[3,48,896]{2,1,0:T(8,128)S(1)}, u32[]{:S(2)}, u32[]{:S(2)}) %collective-permute-start.1) | collective-permute-done | bytes 516128 | tf_op jit(solution)/shard_map/ppermute | solution.py:265
  36.8 0.1 pad_maximum_fusion
  36.9 0.0 copy-start
  36.9 31.5 %all_to_all.20.near_ref = f32[8,48,896]{2,1,0:T(8,128)} all-to-all(f32[8,48,896]{2,1,0:T(8,128)S(1)} %pad_maximum_fusion), channel_id=1, replica_groups=mesh['yh'=2,'z'=8,'yl'=4,'xh'=2,'xl'=2,'c'=2] {'z'}, dimensions={0} | all-to-all | bytes 2752512 | tf_op jit(solution)/shard_map/all_to_all | solution.py:271
  68.4 1.9 %collective-permute-start.2 = (f32[8,48,896]{2,1,0:T(8,128)}, f32[8,48,896]{2,1,0:T(8,128)}, u32[]{:S(2)}, u32[]{:S(2)}) collective-permute-start(f32[8,48,896]{2,1,0:T(8,128)} %all_to_all.20.near_ref), channel_id=1, source_target_pairs={{0,1},{1,0},{2,3},{3,2},{4,5},{5,4},{6,7},{7,6},{8,9},{9,8},{10,11... | collective-permute-start | bytes 4128776 | tf_op jit(solution)/shard_map/ppermute | solution.py:272
  70.3 0.0 copy-done.1
  70.3 0.0 copy-done.5
  70.3 0.0 copy-done
  70.3 2.2 %shard_map.95 = f32[128,4,128]{2,1,0:T(4,128)} custom-call(s32[3]{0:T(128)S(1)} %pad_add_fusion.place_ref, f32[5,45,1440]{2,1,0:T(8,128)S(1)} %copy-done.5, bf16[2,256,1440]{2,1,0:T(8,128)(2,1)S(1)} %copy-done, bf16[2,256,1440]{2,1,0:T(8,128)(2,1)S(1)} %copy-done.1), custom_call_target="tpu_custom_call" | custom-call | flops 600000000 | bytes 3000000 | tf_op jit(solution)/shard_map/pallas_call | solution.py:222
  72.5 13.6 %all-to-all-start.1 = ((f32[128,4,128]{2,1,0:T(4,128)}), f32[128,4,128]{2,1,0:T(4,128)S(1)}, u32[]{:S(2)}, u32[]{:S(2)}) async-start(f32[128,4,128]{2,1,0:T(4,128)} %shard_map.95), calls=%async_computation.1 | async-start | bytes 524288 | tf_op jit(solution)/shard_map/all_to_all | solution.py:288
  86.1 3.3 %copy.13.w_ref = f32[720,2,160]{2,1,0:T(2,128)} copy(f32[720,2,160]{0,2,1:T(8,128)} %param.10) | data formatting | bytes 1843200 | tf_op args[2]
  89.5 1.4 copy-done.2
  90.8 10.8 %shard_map.98.w_ref = f32[80,720]{1,0:T(8,128)S(1)} custom-call(s32[3]{0:T(128)S(1)} %pad_add_fusion.place_ref, s32[1,80]{1,0:T(1,128)S(1)} %slice.25.slots_ref, f32[720,2,160]{2,1,0:T(2,128)S(1)} %copy-done.2), custom_call_target="tpu_custom_call" | custom-call | flops 200000000 | bytes 2000000 | tf_op jit(solution)/shard_map/pallas_call | solution.py:222
  101.6 0.0 copy-start.10
  101.6 0.7 copy-done.10
  102.3 0.0 collective-permute-done.2.far_ref
  102.3 3.3 %shard_map.97 = (bf16[768,720]{1,0:T(8,128)(2,1)S(1)}, bf16[768,720]{1,0:T(8,128)(2,1)S(1)}, f32[80,720]{1,0:T(8,128)S(1)}) custom-call(s32[3]{0:T(128)S(1)} %pad_add_fusion.place_ref, f32[8,48,896]{2,1,0:T(8,128)} %all_to_all.20.near_ref, f32[8,48,896]{2,1,0:T(8,128)} %collective-permute-done.2.far_ref), custom_call_target="tpu_custom_call" | custom-call | flops 100000000 | bytes 6000000 | tf_op jit(solution)/shard_map/pallas_call | solution.py:222
  105.7 0.0 copy-start.6
  105.7 1.0 copy-done.6
  106.7 1.0 copy-done.8
  107.7 0.7 copy-done.14
  108.4 0.0 all-to-all-done.1.x_ref
  108.4 1.3 copy-done.7
  109.7 1.3 copy-done.9
  111.0 0.9 copy-done.11
  111.9 0.9 copy-done.15
  112.9 2.7 %shard_map.99 = f32[128,8,128]{2,1,0:T(8,128)S(1)} custom-call(s32[3]{0:T(128)S(1)} %pad_add_fusion.place_ref, f32[128,4,128]{2,1,0:T(4,128)S(1)} %all-to-all-done.1.x_ref, bf16[768,720]{1,0:T(8,128)(2,1)S(1)} %copy-done.7, bf16[768,720]{1,0:T(8,128)(2,1)S(1)} %copy-done.9, f32[80,720]{1,0:T(8,128)S(1)} %copy-done.15, f32[80,720]{1,0:T(8,128)S(1)} %copy-done.11), custom_call_target="tpu_custom_call" | custom-call | flops 600000000 | bytes 4000000 | tf_op jit(solution)/shard_map/pallas_call | solution.py:222
  115.6 0.0 copy-start.16
  115.6 34.8 %all_to_all.21.x_ref.refs_0_ = f32[128,8,128]{2,1,0:T(8,128)S(1)} all-to-all(f32[128,8,128]{2,1,0:T(8,128)S(1)} %shard_map.99), channel_id=1, replica_groups=mesh['yh'=2,'z'=8,'yl'=4,'xh'=2,'xl'=2,'c'=2] {'yh','z','yl','xh'}, dimensions={0} | all-to-all | bytes 1048576 | tf_op jit(solution)/shard_map/all_to_all | solution.py:313
  150.4 1.3 shard_map.101
  151.7 0.8 copy-done.3
  152.5 6.5 %all-to-all-start.3 = ((f32[32,4,128]{2,1,0:T(4,128)}), f32[32,4,128]{2,1,0:T(4,128)S(1)}, u32[]{:S(2)}, u32[]{:S(2)}) async-start(f32[32,4,128]{2,1,0:T(4,128)} %shard_map.101), calls=%async_computation.3 | async-start | bytes 131072 | tf_op jit(solution)/shard_map/all_to_all | solution.py:316
  159.0 0.1 copy.14.lw_ref
  159.1 1.0 copy-done.4
  160.2 2.6 %shard_map.100 = f32[5,45,1440]{2,1,0:T(8,128)} custom-call(s32[3]{0:T(128)S(1)} %pad_add_fusion.place_ref, f32[128,8,128]{2,1,0:T(8,128)S(1)} %copy-done.4, bf16[2,256,1440]{2,1,0:T(8,128)(2,1)S(1)} %copy-done, bf16[2,256,1440]{2,1,0:T(8,128)(2,1)S(1)} %copy-done.1, f32[45,1]{1,0:T(8,128)S(1)} %copy.14.lw_ref), custom_call_target="tpu_custom_call" | custom-call | flops 600000000 | bytes 4000000 | tf_op jit(solution)/shard_map/pallas_call | solution.py:222
  162.7 4.1 %all-to-all-done.3 = f32[32,4,128]{2,1,0:T(4,128)S(1)} async-done(((f32[32,4,128]{2,1,0:T(4,128)}), f32[32,4,128]{2,1,0:T(4,128)S(1)}, u32[]{:S(2)}, u32[]{:S(2)}) %all-to-all-start.3) | async-done | bytes 65568 | tf_op jit(solution)/shard_map/all_to_all | solution.py:316
  166.9 0.1 reshape_reshape.3
  166.9 0.1 reshape.14
  167.1 0.1 copy.16
  167.2 0.8 copy.17
  (18 shorter events, 0.1 us)
Async XLA Ops:
  1.4 1.0 copy-start.12
  2.4 1.0 copy-start.13
  5.7 17.5 %collective-permute-start = (f32[3,48,896]{2,1,0:T(8,128)S(1)}, f32[3,48,896]{2,1,0:T(8,128)S(1)}, u32[]{:S(2)}, u32[]{:S(2)}) collective-permute-start(f32[3,48,896]{2,1,0:T(8,128)S(1)} %get-tuple-element.9), channel_id=1, source_target_pairs={{0,0},{1,256},{256,1},{257,257},{2,2},{3,258},{258,3},{259,259},{4... | collective-permute-start | bytes 1548296 | tf_op jit(solution)/shard_map/ppermute | solution.py:264
  14.5 22.2 %collective-permute-start.1 = (f32[3,48,896]{2,1,0:T(8,128)S(1)}, f32[3,48,896]{2,1,0:T(8,128)S(1)}, u32[]{:S(2)}, u32[]{:S(2)}) collective-permute-start(f32[3,48,896]{2,1,0:T(8,128)S(1)} %get-tuple-element.10), channel_id=1, source_target_pairs={{0,2},{1,258},{2,0},{3,256},{256,3},{257,259},{258,1},{259,257},{4... | collective-permute-start | bytes 1548296 | tf_op jit(solution)/shard_map/ppermute | solution.py:265
  36.8 33.5 %copy-start.1 = (bf16[2,256,1440]{2,1,0:T(8,128)(2,1)S(1)}, bf16[2,256,1440]{2,1,0:T(8,128)(2,1)}, u32[]{:S(2)}) copy-start(bf16[2,256,1440]{2,1,0:T(8,128)(2,1)} %constant.35.clone.tl_ref) | copy-start | bytes 4423684
  36.8 33.5 %copy-start.5 = (f32[5,45,1440]{2,1,0:T(8,128)S(1)}, f32[5,45,1440]{2,1,0:T(8,128)}, u32[]{:S(2)}) copy-start(f32[5,45,1440]{2,1,0:T(8,128)} %g_ref.1) | copy-start | bytes 3888004
  36.9 33.4 %copy-start = (bf16[2,256,1440]{2,1,0:T(8,128)(2,1)S(1)}, bf16[2,256,1440]{2,1,0:T(8,128)(2,1)}, u32[]{:S(2)}) copy-start(bf16[2,256,1440]{2,1,0:T(8,128)(2,1)} %constant.34.clone.th_ref) | copy-start | bytes 4423684
  68.4 34.0 %collective-permute-start.2 = (f32[8,48,896]{2,1,0:T(8,128)}, f32[8,48,896]{2,1,0:T(8,128)}, u32[]{:S(2)}, u32[]{:S(2)}) collective-permute-start(f32[8,48,896]{2,1,0:T(8,128)} %all_to_all.20.near_ref), channel_id=1, source_target_pairs={{0,1},{1,0},{2,3},{3,2},{4,5},{5,4},{6,7},{7,6},{8,9},{9,8},{10,11... | collective-permute-start | bytes 4128776 | tf_op jit(solution)/shard_map/ppermute | solution.py:272
  72.5 35.9 %all-to-all-start.1 = ((f32[128,4,128]{2,1,0:T(4,128)}), f32[128,4,128]{2,1,0:T(4,128)S(1)}, u32[]{:S(2)}, u32[]{:S(2)}) async-start(f32[128,4,128]{2,1,0:T(4,128)} %shard_map.95), calls=%async_computation.1 | async-start | bytes 524288 | tf_op jit(solution)/shard_map/all_to_all | solution.py:288
  89.5 1.4 copy-start.2
  101.6 0.7 copy-start.10
  105.7 1.0 copy-start.6
  106.7 1.0 copy-start.8
  107.7 0.7 copy-start.14
  108.4 1.3 copy-start.7
  109.7 1.3 copy-start.9
  111.0 0.9 copy-start.11
  111.9 0.9 copy-start.15
  115.6 43.4 %copy-start.16 = (f32[45]{0:T(128)S(1)}, f32[45]{0:T(128)}, u32[]{:S(2)}) copy-start(f32[45]{0:T(128)} %param.12) | copy-start | bytes 544
  151.7 0.8 copy-start.3
  152.5 14.4 %all-to-all-start.3 = ((f32[32,4,128]{2,1,0:T(4,128)}), f32[32,4,128]{2,1,0:T(4,128)S(1)}, u32[]{:S(2)}, u32[]{:S(2)}) async-start(f32[32,4,128]{2,1,0:T(4,128)} %shard_map.101), calls=%async_computation.3 | async-start | bytes 131072 | tf_op jit(solution)/shard_map/all_to_all | solution.py:316
  159.1 1.0 copy-start.4

commit v3 on v0

v3 whole, which is shorter than its diff:
```python
import functools
import math

import jax
import jax.numpy as jnp
import ml_dtypes
import numpy as np
from jax import lax
from jax.experimental import pallas as pl
from jax.experimental.pallas import tpu as pltpu
from jax.sharding import Mesh, PartitionSpec as P

NAMES = ("yh", "zh", "zl", "yl", "x", "c")
SIZES = (2, 4, 2, 4, 4, 2)
LAT = ("yh", "zh", "zl")
LON = ("yl", "x", "c")
GROUP = ("yh", "zh", "yl", "x")
BF = jnp.bfloat16
F32 = jnp.float32
WIDE = 48
HALF = WIDE // 2
SAVED = 768
PICK = (((0,), (1,)), ((), ()))
NN = (((1,), (0,)), ((), ()))
NT = (((1,), (1,)), ((), ()))
TN = (((0,), (0,)), ((), ()))


@functools.cache
def tables(points):
    yh, zh, yl, x = (n.reshape(-1) for n in np.meshgrid(*map(np.arange, (2, 4, 4, 4)), indexing="ij"))
    m = 3 * ((yl * 4 + x) * 2 + yh) + zh
    phase = (m[:, None] * np.arange(points)[None]) % points
    angle = 2.0 * math.pi / points * phase
    rows = np.stack([np.cos(angle), -np.sin(angle)]) / math.sqrt(points)
    full = np.where(zh[None, :, None] < 3, rows, 0.0).reshape(256, points).astype(np.float32)
    high = full.astype(ml_dtypes.bfloat16)
    low = (full - high.astype(np.float32)).astype(ml_dtypes.bfloat16)
    return high, low


def channel_slots(channels):
    per = channels // 32
    c, j, b = np.meshgrid(np.arange(2), np.arange(per), np.arange(16), indexing="ij")
    return ((b * 2 + c) * per + j).reshape(2, channels // 2).astype(np.int32)


def dot(a, b, dims):
    return lax.dot_general(a, b, dims, preferred_element_type=F32)


def two(x):
    high = x.astype(BF)
    return high, (x - high.astype(F32)).astype(BF)


def three(x):
    high, rest = x.astype(BF), None
    rest = x - high.astype(F32)
    mid = rest.astype(BF)
    return high, mid, (rest - mid.astype(F32)).astype(BF)


def prepare_kernel(leg_ref, saved_ref, out_ref):
    orders, rows, degrees = leg_ref.shape
    channels = saved_ref.shape[3]
    out_ref[...] = jnp.zeros_like(out_ref)
    for side in range(2):
        n = min(HALF, rows - side * HALF)
        at = slice(side * HALF, side * HALF + n)
        for k in range(orders):
            out_ref[side, k, :n, :degrees] = leg_ref[k, at, :]
            for r in range(2):
                lane = SAVED + r * channels
                out_ref[side, k, :n, lane : lane + channels] = saved_ref[at, k, r, :]


def picks(slots_ref, channels):
    n = slots_ref.shape[1]
    return (lax.broadcasted_iota(jnp.int32, (channels, n), 0) == slots_ref[...]).astype(F32).astype(BF)


def weight_kernel(slots_ref, w_ref, out_ref):
    _, channels, _ = w_ref.shape
    half = channels // 2
    pick = picks(slots_ref, channels)
    for r in range(2):
        out_ref[r * half : (r + 1) * half, :] = sum(dot(pick, term, TN) for term in three(w_ref[r]))


def forward_kernel(g_ref, th_ref, tl_ref, out_ref, field):
    group, rows, points = g_ref.shape
    field[...] = jnp.zeros_like(field)
    for j in range(group):
        field[j * WIDE : j * WIDE + rows, :] = g_ref[j]
    high, low = two(field[...])
    table = th_ref[...]
    acc = dot(table, high, NT) + dot(table, low, NT) + dot(tl_ref[...], high, NT)
    for r in range(2):
        for k in range(2):
            out_ref[:, 2 * r + k, :] = acc[r * 128 : (r + 1) * 128, k * 128 : (k + 1) * 128]


def split_kernel(place_ref, slots_ref, near_ref, far_ref, lh_ref, ll_ref, sv_ref, both):
    degrees = lh_ref.shape[1]
    half = sv_ref.shape[0] // 2
    channels = 2 * half
    rows = degrees // 16
    c = place_ref[0]
    both[:, pl.ds(pl.multiple_of(c * HALF, HALF), HALF), :] = near_ref[...]
    both[:, pl.ds(pl.multiple_of((1 - c) * HALF, HALF), HALF), :] = far_ref[...]
    high, low = two(both[:, :, :degrees].reshape(8 * WIDE, degrees))
    lh_ref[...] = high
    ll_ref[...] = low
    pick = picks(slots_ref, channels)
    for r in range(2):
        lane = SAVED + r * channels
        v = both[:, :, lane : lane + channels].reshape(8 * WIDE, channels)
        mine = sum(dot(pick, term, PICK) for term in three(v))
        for a in range(8):
            piece = mine[:, a * WIDE : a * WIDE + rows]
            for side in range(2):
                at = (2 * a + side) * rows
                sv_ref[r * half : (r + 1) * half, at : at + rows] = piece


def analysis_kernel(x_ref, lh_ref, ll_ref, out_ref, ct, tmp):
    for k in range(4):
        tmp[:, k * 128 : (k + 1) * 128] = x_ref[:, k, :]
    for a in range(8):
        for r in range(2):
            for j in range(5):
                q = (r * 5 + j) * 16
                lane = r * 256 + j * WIDE
                ct[q : q + 16, a * WIDE : (a + 1) * WIDE] = tmp[a * 16 : a * 16 + 16, lane : lane + WIDE]
    ch, cl = two(ct[...])
    n = ch.shape[0]
    both = dot(jnp.concatenate([ch, cl], axis=0), lh_ref[...], NN)
    out_ref[...] = both[:n] + both[n:] + dot(ch, ll_ref[...], NN)


def synthesis_kernel(place_ref, near_ref, far_ref, lh_ref, ll_ref, sv_ref, w_ref, out_ref, back):
    half, degrees = sv_ref.shape[0] // 2, sv_ref.shape[1]
    n, rows = 2 * half, degrees // 16
    back[...] = jnp.zeros_like(back)
    spec = near_ref[...] + far_ref[...]
    g, h = spec[:half], spec[half:]
    u, v = w_ref[:half, :], w_ref[half:, :]
    twice = jnp.where(place_ref[2] == 1, 1.0, 2.0).astype(F32)
    adjoint = jnp.concatenate([(u * g + v * h) * twice, (u * h - v * g) * twice], axis=0)
    p, q = sv_ref[:half, :], sv_ref[half:, :]
    part = (p * g + q * h, p * h - q * g)
    ah, al = two(adjoint)
    both = dot(jnp.concatenate([ah, al], axis=0), lh_ref[...], NT)
    syn = both[:n] + both[n:] + dot(ah, ll_ref[...], NT)
    zl = place_ref[1]
    for a in range(8):
        to = slice(a * 16, a * 16 + 16)
        for r in range(2):
            for j in range(5):
                at = (r * 5 + j) * 16
                lane = r * 256 + j * WIDE
                back[to, lane : lane + WIDE] = syn[at : at + 16, a * WIDE : (a + 1) * WIDE]
                pair = part[r][j * 16 : j * 16 + 16, 2 * a * rows : (2 * a + 2) * rows]
                back[to, 512 + lane : 512 + lane + rows] = jnp.where(zl == 0, pair[:, :rows], pair[:, rows:])
    for k in range(8):
        out_ref[:, k, :] = back[:, k * 128 : (k + 1) * 128]


def share_kernel(x_ref, out_ref):
    total = jnp.sum(x_ref[...], axis=0)[4:8]
    out_ref[...] = jnp.broadcast_to(total[None], out_ref.shape)


def inverse_kernel(x_ref, th_ref, tl_ref, lw_ref, out_ref):
    group, rows, points = out_ref.shape
    block = jnp.concatenate(
        [jnp.concatenate([x_ref[:, 2 * r, :], x_ref[:, 2 * r + 1, :]], axis=1) for r in range(2)], axis=0
    )
    high, low = two(block)
    table = th_ref[...]
    acc = dot(high, table, TN) + dot(low, table, TN) + dot(high, tl_ref[...], TN)
    for j in range(group):
        out_ref[j] = acc[j * WIDE : j * WIDE + rows] * lw_ref[...]


def call(kernel, args, out_shapes, flops, scratch=(), scalars=0, hbm_out=False):
    vmem = pl.BlockSpec(memory_space=pltpu.VMEM)
    smem = pl.BlockSpec(memory_space=pltpu.SMEM)
    moved = sum(a.size * a.dtype.itemsize for a in (*args, *jax.tree.leaves(out_shapes)))
    extra = {} if hbm_out else dict(out_specs=jax.tree.map(lambda s: vmem, out_shapes))
    return pl.pallas_call(
        kernel,
        out_shape=out_shapes,
        in_specs=[smem if i < scalars else vmem for i in range(len(args))],
        scratch_shapes=list(scratch),
        compiler_params=pltpu.CompilerParams(vmem_limit_bytes=24 * 2**20),
        cost_estimate=pl.CostEstimate(flops=flops, bytes_accessed=moved, transcendentals=0),
        **extra,
    )(*args)


def shape(*dims, dtype=F32):
    return jax.ShapeDtypeStruct(dims, dtype)


def local(grad_out, saved_spectra, spec_weight, legendre, lat_weight):
    group, rows, points = grad_out.shape
    degrees, _, channels = spec_weight.shape
    orders = legendre.shape[0]
    half = channels // 2
    yh, zh, zl, yl, x, c = (lax.axis_index(n) for n in NAMES)
    first = yh + zh + yl + x == 0
    place = jnp.stack([c, zl, first.astype(jnp.int32)]).astype(jnp.int32)
    slot_table = jnp.asarray(channel_slots(channels))
    slots = jnp.where(c == 0, slot_table[0:1], slot_table[1:2])
    high, low = (jnp.asarray(t) for t in tables(points))

    rows_out = call(
        prepare_kernel,
        (legendre, saved_spectra),
        shape(2, orders + 1, HALF, SAVED + 3 * 128),
        1000,
    )
    rows_out = lax.all_to_all(rows_out, ("c",), 0, 0, tiled=True)
    near = lax.all_to_all(rows_out.reshape(8, HALF, -1), ("yh", "zh"), 0, 0, tiled=True)

    coeffs = call(
        forward_kernel,
        (grad_out, high, low),
        shape(128, 4, 128),
        600_000_000,
        scratch=[pltpu.VMEM((256, points), F32)],
    )
    weight = call(weight_kernel, (slots, spec_weight.transpose(1, 2, 0)), shape(2 * half, degrees), 100_000_000)
    coeffs, weight, near = lax.optimization_barrier((coeffs, weight, near))
    far = lax.ppermute(near, ("c",), [(0, 1), (1, 0)])
    coeffs = lax.all_to_all(coeffs, GROUP, 0, 0, tiled=True)
    leg_high, leg_low, sv = call(
        split_kernel,
        (place, slots, near, far),
        (
            shape(8 * WIDE, degrees, dtype=BF),
            shape(8 * WIDE, degrees, dtype=BF),
            shape(2 * half, degrees),
        ),
        100_000_000,
        scratch=[pltpu.VMEM((8, WIDE, SAVED + 3 * 128), F32)],
        scalars=1,
    )
    spectra = call(
        analysis_kernel,
        (coeffs, leg_high, leg_low),
        shape(2 * half, degrees),
        300_000_000,
        scratch=[pltpu.VMEM((2 * half, 8 * WIDE), F32), pltpu.VMEM((128, 512), F32)],
    )
    other = lax.ppermute(spectra, ("zl",), [(0, 1), (1, 0)])
    back = call(
        synthesis_kernel,
        (place, spectra, other, leg_high, leg_low, sv, weight),
        shape(128, 8, 128),
        300_000_000,
        scratch=[pltpu.VMEM((128, 1024), F32)],
        scalars=1,
    )
    back = lax.all_to_all(back, GROUP, 0, 0, tiled=True)

    share = call(share_kernel, (back,), shape(32, 4, 128), 1_000_000)
    share = lax.all_to_all(share, LON, 0, 0, tiled=True)
    grad_in = call(
        inverse_kernel,
        (back, high, low, lat_weight.reshape(rows, 1)),
        shape(group, rows, points),
        600_000_000,
        hbm_out=True,
    )
    grad_weight = share.reshape(32, 2, 256)[..., : group * WIDE].reshape(32, 2, group, WIDE)[..., :rows]
    grad_weight = grad_weight.transpose(3, 1, 0, 2).reshape(rows, 2, channels)
    return (grad_in, grad_weight)


def solution(mesh):
    fine = Mesh(mesh.devices.reshape(SIZES), NAMES)
    return jax.shard_map(
        local,
        mesh=fine,
        in_specs=(P(LON, LAT, None), P(LAT, LON, None, None), P(), P(LON, LAT, None), P(LAT)),
        out_specs=(P(LON, LAT, None), P(LAT, None, None)),
        check_vma=False,
    )
```

time: 429 us -> 150 us (0.35)
  waiting for transfers between devices: 219 us -> 45.7 us
  blocking collectives: 153 us -> 37.9 us
  starting transfers between devices: 8.69 us -> 44.5 us
  between operations: 14.3 us -> 0.85 us
  Pallas kernels: 0 us -> 13 us
  matrix products: 11.3 us -> 0 us
  other arithmetic: 10.5 us -> 0.08 us
    psum x1 -> x0, waiting for transfers between devices: 219 us -> none  [local(): spectra = lax.psum(partial_terms, 'lat')]
    psum x1 -> x0, blocking collectives: 134 us -> none  [local(): grad_weight = lax.psum(weight_part, 'lon')]
    all_to_all x1 -> x3, waiting for transfers between devices: 0.01 us -> 35.4 us  [the longest x1 17.5 us: local(): lax.all_to_all(rows_out.reshape(8, HALF, -1), ('yh', 'zh'), 0, 0, tiled=T...]
    all_to_all x1 -> x3, starting transfers between devices: 8.65 us -> 36.5 us  [the longest x1 19.2 us: local(): coeffs = lax.all_to_all(coeffs, GROUP, 0, 0, tiled=True)]
    all_to_all x1 -> x2, blocking collectives: 18.9 us -> 37.9 us  [the longest x1 26.2 us: local(): back = lax.all_to_all(back, GROUP, 0, 0, tiled=True)]
    pallas_call x0 -> x8, Pallas kernels: none -> 13 us  [call(): pl.pallas_call(kernel, out_shape=out_shapes, in_specs=[smem if i < scalar...]
    dot_general x4 -> x0, matrix products: 11.3 us -> none  [the longest x1 4.07 us: local(): jnp.einsum('ipl,cpri->lirc', legendre, by_order, precision=lax.Precision....]
    ppermute x0 -> x2, waiting for transfers between devices: none -> 10.3 us  [the longest x1 10.3 us: local(): other = lax.ppermute(spectra, ('zl',), [(0, 1), (1, 0)])]
  transfers between devices with their start and end apart: 2 -> 5, of which waited for: 1 -> 4; matrix products, arithmetic and copies ran while one was open for 1% -> 0% of each run, Pallas kernels for 0% -> 4%
where the time goes in v3:
time: 150 us; the launch traced here: 149 us
  waiting for transfers between devices  45.7 us (30%)
  starting transfers between devices  44.5 us (30%)
  blocking collectives  37.9 us (25%)
  Pallas kernels  13 us (9%)
  local copies, waits for them, and re-layouts  7.15 us (5%)
    all_to_all x1, blocking collectives, local(): back = lax.all_to_all(back, GROUP, 0, 0, tiled=True)  26.2 us
    all_to_all x1, starting transfers between devices, local(): coeffs = lax.all_to_all(coeffs, GROUP, 0, 0, tiled=True)  19.2 us
    all_to_all x1, waiting for transfers between devices, local(): lax.all_to_all(rows_out.reshape(8, HALF, -1), ('yh', 'zh'), 0, 0, tiled=T...  17.5 us
    pallas_call x8, Pallas kernels, call(): pl.pallas_call(kernel, out_shape=out_shapes, in_specs=[smem if i < scalar...  13 us
    all_to_all x1, waiting for transfers between devices, local(): coeffs = lax.all_to_all(coeffs, GROUP, 0, 0, tiled=True)  12.2 us
    all_to_all x1, blocking collectives, local(): rows_out = lax.all_to_all(rows_out, ('c',), 0, 0, tiled=True)  11.7 us
    ppermute x1, waiting for transfers between devices, local(): other = lax.ppermute(spectra, ('zl',), [(0, 1), (1, 0)])  10.3 us
    all_to_all x1, starting transfers between devices, local(): lax.all_to_all(rows_out.reshape(8, HALF, -1), ('yh', 'zh'), 0, 0, tiled=T...  10 us
  transfers between devices with their start and end apart: 5, of which 4 were waited for; matrix products, arithmetic and copies ran while one was open for 0% of the time, Pallas kernels for 4%

profile of v3, /device:TPU:1, one launch (start us, length us, event | category | flops | bytes accessed | tf_op | source)
XLA Modules:
  0.0 149.1 jit_solution(4573659347045180751)
XLA Ops:
  0.6 0.0 copy-start.9
  0.6 1.0 copy-done.9
  1.6 0.0 copy-start.10
  1.6 1.0 copy-done.10
  2.6 0.1 shard_map.97
  2.7 0.0 copy-start.12
  2.8 0.0 copy-start.13
  2.8 11.7 %all_to_all.25 = f32[2,4,24,1152]{3,2,1,0:T(8,128)} all-to-all(f32[2,4,24,1152]{3,2,1,0:T(8,128)S(1)} %shard_map.97), channel_id=1, replica_groups=mesh['yh'=2,'zh'=4,'zl'=2,'yl'=4,'x'=4,'c'=2] {'c'}, dimensions={0} | all-to-all | bytes 1769472 | tf_op jit(solution)/shard_map/all_to_all | solution.py:225
  14.5 10.0 %all-to-all-start.1 = ((f32[8,24,1152]{2,1,0:T(8,128)}), f32[8,24,1152]{2,1,0:T(8,128)S(1)}, u32[]{:S(2)}, u32[]{:S(2)}) async-start(f32[8,24,1152]{2,1,0:T(8,128)} %bitcast.4), calls=%async_computation.1 | async-start | bytes 1769472 | tf_op jit(solution)/shard_map/all_to_all | solution.py:226
  24.5 0.0 copy-done.12
  24.5 0.0 copy-done.13
  24.6 0.0 copy-start.5
  24.6 0.0 copy-start.6
  24.6 1.3 copy-done.6
  25.9 0.4 shard_map.96.w_ref
  26.3 0.0 copy-done
  26.4 0.0 copy-done.1
  26.4 0.0 copy-done.5
  26.4 1.7 %shard_map.95 = f32[128,4,128]{2,1,0:T(4,128)} custom-call(f32[5,45,1440]{2,1,0:T(8,128)S(1)} %copy-done.5, bf16[256,1440]{1,0:T(8,128)(2,1)S(1)} %copy-done, bf16[256,1440]{1,0:T(8,128)(2,1)S(1)} %copy-done.1), custom_call_target="tpu_custom_call" | custom-call | flops 600000000 | bytes 3032704 | tf_op jit(solution)/shard_map/pallas_call | solution.py:192
  28.0 17.5 %all-to-all-done.1.near_ref = f32[8,24,1152]{2,1,0:T(8,128)S(1)} async-done(((f32[8,24,1152]{2,1,0:T(8,128)}), f32[8,24,1152]{2,1,0:T(8,128)S(1)}, u32[]{:S(2)}, u32[]{:S(2)}) %all-to-all-start.1) | async-done | bytes 884768 | tf_op jit(solution)/shard_map/all_to_all | solution.py:226
  45.6 5.3 %collective-permute-start = (f32[8,24,1152]{2,1,0:T(8,128)S(1)}, f32[8,24,1152]{2,1,0:T(8,128)}, u32[]{:S(2)}, u32[]{:S(2)}) collective-permute-start(f32[8,24,1152]{2,1,0:T(8,128)S(1)} %all-to-all-done.1.near_ref), channel_id=1, source_target_pairs={{0,1},{1,0},{2,3},{3,2},{4,5},{5,4},{6,7},{7,6},{8,9},{9,8},{10,11... | collective-permute-start | bytes 2654216 | tf_op jit(solution)/shard_map/ppermute | solution.py:237
  50.9 19.2 %all-to-all-start.2 = ((f32[128,4,128]{2,1,0:T(4,128)}), f32[128,4,128]{2,1,0:T(4,128)}, u32[]{:S(2)}, u32[]{:S(2)}) async-start(f32[128,4,128]{2,1,0:T(4,128)} %shard_map.95), calls=%async_computation.2 | async-start | bytes 524288 | tf_op jit(solution)/shard_map/all_to_all | solution.py:238
  70.1 0.1 pad_add_fusion.place_ref
  70.1 0.0 collective-permute-done.far_ref
  70.1 2.4 %shard_map.98 = (bf16[384,720]{1,0:T(8,128)(2,1)S(1)}, bf16[384,720]{1,0:T(8,128)(2,1)S(1)}, f32[160,720]{1,0:T(8,128)S(1)}) custom-call(s32[3]{0:T(128)S(1)} %pad_add_fusion.place_ref, s32[1,80]{1,0:T(1,128)S(1)} %broadcast_select_fusion.slots_ref, f32[8,24,1152]{2,1,0:T(8,128)S(1)} %all-to-all-done.1.near_ref, f32[8,24,1152]{2,1,0:T(8,128)} %collective-permute-done.far_ref), custom_call_target="tpu_custom_call" | custom-call | flops 100000000 | bytes 3336524 | tf_op jit(solution)/shard_map/pallas_call | solution.py:192
  72.6 0.0 copy-start.2
  72.6 0.8 copy-done.2
  73.4 0.8 copy-done.7
  74.2 12.2 %all-to-all-done.2.x_ref = f32[128,4,128]{2,1,0:T(4,128)} async-done(((f32[128,4,128]{2,1,0:T(4,128)}), f32[128,4,128]{2,1,0:T(4,128)}, u32[]{:S(2)}, u32[]{:S(2)}) %all-to-all-start.2) | async-done | bytes 262176 | tf_op jit(solution)/shard_map/all_to_all | solution.py:238
  86.3 1.1 copy-done.3
  87.4 1.8 %shard_map.99.near_ref = f32[160,720]{1,0:T(8,128)S(1)} custom-call(f32[128,4,128]{2,1,0:T(4,128)} %all-to-all-done.2.x_ref, bf16[384,720]{1,0:T(8,128)(2,1)S(1)} %get-tuple-element.10.lh_ref, bf16[384,720]{1,0:T(8,128)(2,1)S(1)} %copy-done.3), custom_call_target="tpu_custom_call" | custom-call | flops 300000000 | bytes 1828864 | tf_op jit(solution)/shard_map/pallas_call | solution.py:192
  89.2 2.7 %collective-permute-start.1 = (f32[160,720]{1,0:T(8,128)S(1)}, f32[160,720]{1,0:T(8,128)S(1)}, u32[]{:S(2)}, u32[]{:S(2)}) collective-permute-start(f32[160,720]{1,0:T(8,128)S(1)} %shard_map.99.near_ref), channel_id=1, source_target_pairs={{0,32},{32,0},{1,33},{33,1},{2,34},{34,2},{3,35},{35,3},{4,36},{36... | collective-permute-start | bytes 1382408 | tf_op jit(solution)/shard_map/ppermute | solution.py:258
  91.9 10.3 %collective-permute-done.1.far_ref = f32[160,720]{1,0:T(8,128)S(1)} collective-permute-done((f32[160,720]{1,0:T(8,128)S(1)}, f32[160,720]{1,0:T(8,128)S(1)}, u32[]{:S(2)}, u32[]{:S(2)}) %collective-permute-start.1) | collective-permute-done | bytes 460832 | tf_op jit(solution)/shard_map/ppermute | solution.py:258
  102.2 0.0 copy-done.4
  102.2 0.0 copy-done.8
  102.2 3.7 %shard_map.100 = f32[128,8,128]{2,1,0:T(8,128)S(1)} custom-call(s32[3]{0:T(128)S(1)} %pad_add_fusion.place_ref, f32[160,720]{1,0:T(8,128)S(1)} %shard_map.99.near_ref, f32[160,720]{1,0:T(8,128)S(1)} %collective-permute-done.1.far_ref, bf16[384,720]{1,0:T(8,128)(2,1)S(1)} %get-tuple-element.10.lh_ref, bf16[384,720]{1,0:T(8,128)(2,1)S(1)} %copy-done.4, ...), custom_call_target="tpu_custom_call" | custom-call | flops 300000000 | bytes 3473420 | tf_op jit(solution)/shard_map/pallas_call | solution.py:192
  105.9 0.0 copy-start.11
  105.9 26.2 %all_to_all.26.x_ref = f32[128,8,128]{2,1,0:T(8,128)S(1)} all-to-all(f32[128,8,128]{2,1,0:T(8,128)S(1)} %shard_map.100), channel_id=1, replica_groups=mesh['yh'=2,'zh'=4,'zl'=2,'yl'=4,'x'=4,'c'=2] {'yh','zh','yl','x'}, dimensions={0} | all-to-all | bytes 1048576 | tf_op jit(solution)/shard_map/all_to_all | solution.py:267
  132.1 0.8 shard_map.102
  132.9 7.3 %all-to-all-start.4 = ((f32[32,4,128]{2,1,0:T(4,128)}), f32[32,4,128]{2,1,0:T(4,128)S(1)}, u32[]{:S(2)}, u32[]{:S(2)}) async-start(f32[32,4,128]{2,1,0:T(4,128)} %shard_map.102), calls=%async_computation.4 | async-start | bytes 131072 | tf_op jit(solution)/shard_map/all_to_all | solution.py:270
  140.2 0.0 copy-done.11
  140.2 0.1 copy.12.lw_ref
  140.3 2.0 %shard_map.101 = f32[5,45,1440]{2,1,0:T(8,128)} custom-call(f32[128,8,128]{2,1,0:T(8,128)S(1)} %all_to_all.26.x_ref, bf16[256,1440]{1,0:T(8,128)(2,1)S(1)} %copy-done, bf16[256,1440]{1,0:T(8,128)(2,1)S(1)} %copy-done.1, f32[45,1]{1,0:T(8,128)S(1)} %copy.12.lw_ref), custom_call_target="tpu_custom_call" | custom-call | flops 600000000 | bytes 3295028 | tf_op jit(solution)/shard_map/pallas_call | solution.py:192
  142.3 5.7 %all-to-all-done.4 = f32[32,4,128]{2,1,0:T(4,128)S(1)} async-done(((f32[32,4,128]{2,1,0:T(4,128)}), f32[32,4,128]{2,1,0:T(4,128)S(1)}, u32[]{:S(2)}, u32[]{:S(2)}) %all-to-all-start.4) | async-done | bytes 65568 | tf_op jit(solution)/shard_map/all_to_all | solution.py:270
  148.0 0.1 reshape.21
  148.1 0.1 reshape.22
  148.2 0.1 copy.14
  148.4 0.8 copy.15
  (9 shorter events, 0.0 us)
Async XLA Ops:
  0.6 1.0 copy-start.9
  1.6 1.0 copy-start.10
  2.7 21.8 %copy-start.12 = (s32[1,80]{1,0:T(1,128)S(1)}, s32[1,80]{1,0:T(1,128)}, u32[]{:S(2)}) copy-start(s32[1,80]{1,0:T(1,128)} %constant.38) | copy-start | bytes 964
  2.8 21.8 %copy-start.13 = (s32[1,80]{1,0:T(1,128)S(1)}, s32[1,80]{1,0:T(1,128)}, u32[]{:S(2)}) copy-start(s32[1,80]{1,0:T(1,128)} %constant.39) | copy-start | bytes 964
  14.5 11.9 %copy-start = (bf16[256,1440]{1,0:T(8,128)(2,1)S(1)}, bf16[256,1440]{1,0:T(8,128)(2,1)}, u32[]{:S(2)}) copy-start(bf16[256,1440]{1,0:T(8,128)(2,1)} %constant.32.clone.th_ref) | copy-start | bytes 2211844
  14.5 11.9 %copy-start.1 = (bf16[256,1440]{1,0:T(8,128)(2,1)S(1)}, bf16[256,1440]{1,0:T(8,128)(2,1)}, u32[]{:S(2)}) copy-start(bf16[256,1440]{1,0:T(8,128)(2,1)} %constant.33.clone.tl_ref) | copy-start | bytes 2211844
  14.5 31.1 %all-to-all-start.1 = ((f32[8,24,1152]{2,1,0:T(8,128)}), f32[8,24,1152]{2,1,0:T(8,128)S(1)}, u32[]{:S(2)}, u32[]{:S(2)}) async-start(f32[8,24,1152]{2,1,0:T(8,128)} %bitcast.4), calls=%async_computation.1 | async-start | bytes 1769472 | tf_op jit(solution)/shard_map/all_to_all | solution.py:226
  24.6 1.8 %copy-start.5 = (f32[5,45,1440]{2,1,0:T(8,128)S(1)}, f32[5,45,1440]{2,1,0:T(8,128)}, u32[]{:S(2)}) copy-start(f32[5,45,1440]{2,1,0:T(8,128)} %g_ref.1) | copy-start | bytes 3888004
  24.6 1.3 copy-start.6
  45.6 24.6 %collective-permute-start = (f32[8,24,1152]{2,1,0:T(8,128)S(1)}, f32[8,24,1152]{2,1,0:T(8,128)}, u32[]{:S(2)}, u32[]{:S(2)}) collective-permute-start(f32[8,24,1152]{2,1,0:T(8,128)S(1)} %all-to-all-done.1.near_ref), channel_id=1, source_target_pairs={{0,1},{1,0},{2,3},{3,2},{4,5},{5,4},{6,7},{7,6},{8,9},{9,8},{10,11... | collective-permute-start | bytes 2654216 | tf_op jit(solution)/shard_map/ppermute | solution.py:237
  50.9 35.5 %all-to-all-start.2 = ((f32[128,4,128]{2,1,0:T(4,128)}), f32[128,4,128]{2,1,0:T(4,128)}, u32[]{:S(2)}, u32[]{:S(2)}) async-start(f32[128,4,128]{2,1,0:T(4,128)} %shard_map.95), calls=%async_computation.2 | async-start | bytes 524288 | tf_op jit(solution)/shard_map/all_to_all | solution.py:238
  72.6 0.8 copy-start.2
  73.4 0.8 copy-start.7
  86.3 1.1 copy-start.3
  87.4 14.8 %copy-start.4 = (bf16[384,720]{1,0:T(8,128)(2,1)S(1)}, bf16[384,720]{1,0:T(8,128)(2,1)}, u32[]{:S(2)}) copy-start(bf16[384,720]{1,0:T(8,128)(2,1)} %copy-done.2) | copy-start | bytes 1658884
  87.4 14.8 %copy-start.8 = (f32[160,720]{1,0:T(8,128)S(1)}, f32[160,720]{1,0:T(8,128)}, u32[]{:S(2)}) copy-start(f32[160,720]{1,0:T(8,128)} %copy-done.7) | copy-start | bytes 1382404
  89.2 13.0 %collective-permute-start.1 = (f32[160,720]{1,0:T(8,128)S(1)}, f32[160,720]{1,0:T(8,128)S(1)}, u32[]{:S(2)}, u32[]{:S(2)}) collective-permute-start(f32[160,720]{1,0:T(8,128)S(1)} %shard_map.99.near_ref), channel_id=1, source_target_pairs={{0,32},{32,0},{1,33},{33,1},{2,34},{34,2},{3,35},{35,3},{4,36},{36... | collective-permute-start | bytes 1382408 | tf_op jit(solution)/shard_map/ppermute | solution.py:258
  105.9 34.3 %copy-start.11 = (f32[45]{0:T(128)S(1)}, f32[45]{0:T(128)}, u32[]{:S(2)}) copy-start(f32[45]{0:T(128)} %param.12) | copy-start | bytes 544
  132.9 15.1 %all-to-all-start.4 = ((f32[32,4,128]{2,1,0:T(4,128)}), f32[32,4,128]{2,1,0:T(4,128)S(1)}, u32[]{:S(2)}, u32[]{:S(2)}) async-start(f32[32,4,128]{2,1,0:T(4,128)} %shard_map.102), calls=%async_computation.4 | async-start | bytes 131072 | tf_op jit(solution)/shard_map/all_to_all | solution.py:270

commit v4 on v3

--- a/solution.py
+++ b/solution.py
@@ -10,11 +10,11 @@
 from jax.experimental.pallas import tpu as pltpu
 from jax.sharding import Mesh, PartitionSpec as P
 
-NAMES = ("yh", "zh", "zl", "yl", "x", "c")
-SIZES = (2, 4, 2, 4, 4, 2)
-LAT = ("yh", "zh", "zl")
+NAMES = ("yh", "z", "yl", "x", "c")
+SIZES = (2, 8, 4, 4, 2)
+LAT = ("yh", "z")
 LON = ("yl", "x", "c")
-GROUP = ("yh", "zh", "yl", "x")
+GROUP = ("z", "yl", "x")
 BF = jnp.bfloat16
 F32 = jnp.float32
 WIDE = 48
@@ -28,12 +28,12 @@
 
 @functools.cache
 def tables(points):
-    yh, zh, yl, x = (n.reshape(-1) for n in np.meshgrid(*map(np.arange, (2, 4, 4, 4)), indexing="ij"))
-    m = 3 * ((yl * 4 + x) * 2 + yh) + zh
+    z, yl, x = (n.reshape(-1) for n in np.meshgrid(*map(np.arange, (8, 4, 4)), indexing="ij"))
+    m = 3 * ((yl * 4 + x) * 2 + z // 4) + z % 4
     phase = (m[:, None] * np.arange(points)[None]) % points
     angle = 2.0 * math.pi / points * phase
     rows = np.stack([np.cos(angle), -np.sin(angle)]) / math.sqrt(points)
-    full = np.where(zh[None, :, None] < 3, rows, 0.0).reshape(256, points).astype(np.float32)
+    full = np.where(z[None, :, None] % 4 < 3, rows, 0.0).reshape(256, points).astype(np.float32)
     high = full.astype(ml_dtypes.bfloat16)
     low = (full - high.astype(np.float32)).astype(ml_dtypes.bfloat16)
     return high, low
@@ -118,10 +118,7 @@
         v = both[:, :, lane : lane + channels].reshape(8 * WIDE, channels)
         mine = sum(dot(pick, term, PICK) for term in three(v))
         for a in range(8):
-            piece = mine[:, a * WIDE : a * WIDE + rows]
-            for side in range(2):
-                at = (2 * a + side) * rows
-                sv_ref[r * half : (r + 1) * half, at : at + rows] = piece
+            sv_ref[r * half : (r + 1) * half, a * rows : (a + 1) * rows] = mine[:, a * WIDE : a * WIDE + rows]
 
 
 def analysis_kernel(x_ref, lh_ref, ll_ref, out_ref, ct, tmp):
@@ -140,7 +137,7 @@
 
 
 def synthesis_kernel(place_ref, near_ref, far_ref, lh_ref, ll_ref, sv_ref, w_ref, out_ref, back):
-    half, degrees = sv_ref.shape[0] // 2, sv_ref.shape[1]
+    half, degrees = w_ref.shape[0] // 2, w_ref.shape[1]
     n, rows = 2 * half, degrees // 16
     back[...] = jnp.zeros_like(back)
     spec = near_ref[...] + far_ref[...]
@@ -149,11 +146,12 @@
     twice = jnp.where(place_ref[2] == 1, 1.0, 2.0).astype(F32)
     adjoint = jnp.concatenate([(u * g + v * h) * twice, (u * h - v * g) * twice], axis=0)
     p, q = sv_ref[:half, :], sv_ref[half:, :]
+    own = jnp.where(place_ref[1] == 0, spec[:, : degrees // 2], spec[:, degrees // 2 :])
+    g, h = own[:half], own[half:]
     part = (p * g + q * h, p * h - q * g)
     ah, al = two(adjoint)
     both = dot(jnp.concatenate([ah, al], axis=0), lh_ref[...], NT)
     syn = both[:n] + both[n:] + dot(ah, ll_ref[...], NT)
-    zl = place_ref[1]
     for a in range(8):
         to = slice(a * 16, a * 16 + 16)
         for r in range(2):
@@ -161,8 +159,8 @@
                 at = (r * 5 + j) * 16
                 lane = r * 256 + j * WIDE
                 back[to, lane : lane + WIDE] = syn[at : at + 16, a * WIDE : (a + 1) * WIDE]
-                pair = part[r][j * 16 : j * 16 + 16, 2 * a * rows : (2 * a + 2) * rows]
-                back[to, 512 + lane : 512 + lane + rows] = jnp.where(zl == 0, pair[:, :rows], pair[:, rows:])
+                piece = part[r][j * 16 : j * 16 + 16, a * rows : (a + 1) * rows]
+                back[to, 512 + lane : 512 + lane + rows] = piece
     for k in range(8):
         out_ref[:, k, :] = back[:, k * 128 : (k + 1) * 128]
 
@@ -209,9 +207,9 @@
     degrees, _, channels = spec_weight.shape
     orders = legendre.shape[0]
     half = channels // 2
-    yh, zh, zl, yl, x, c = (lax.axis_index(n) for n in NAMES)
-    first = yh + zh + yl + x == 0
-    place = jnp.stack([c, zl, first.astype(jnp.int32)]).astype(jnp.int32)
+    yh, z, yl, x, c = (lax.axis_index(n) for n in NAMES)
+    first = z + yl + x == 0
+    place = jnp.stack([c, yh, first.astype(jnp.int32)]).astype(jnp.int32)
     slot_table = jnp.asarray(channel_slots(channels))
     slots = jnp.where(c == 0, slot_table[0:1], slot_table[1:2])
     high, low = (jnp.asarray(t) for t in tables(points))
@@ -223,7 +221,7 @@
         1000,
     )
     rows_out = lax.all_to_all(rows_out, ("c",), 0, 0, tiled=True)
-    near = lax.all_to_all(rows_out.reshape(8, HALF, -1), ("yh", "zh"), 0, 0, tiled=True)
+    near = lax.all_to_all(rows_out.reshape(8, HALF, -1), ("z",), 0, 0, tiled=True)
 
     coeffs = call(
         forward_kernel,
@@ -242,7 +240,7 @@
         (
             shape(8 * WIDE, degrees, dtype=BF),
             shape(8 * WIDE, degrees, dtype=BF),
-            shape(2 * half, degrees),
+            shape(2 * half, degrees // 2),
         ),
         100_000_000,
         scratch=[pltpu.VMEM((8, WIDE, SAVED + 3 * 128), F32)],
@@ -255,7 +253,7 @@
         300_000_000,
         scratch=[pltpu.VMEM((2 * half, 8 * WIDE), F32), pltpu.VMEM((128, 512), F32)],
     )
-    other = lax.ppermute(spectra, ("zl",), [(0, 1), (1, 0)])
+    other = lax.ppermute(spectra, ("yh",), [(0, 1), (1, 0)])
     back = call(
         synthesis_kernel,
         (place, spectra, other, leg_high, leg_low, sv, weight),

time: 150 us -> 145 us (0.967)
  starting transfers between devices: 44.5 us -> 27.8 us
  waiting for transfers between devices: 45.7 us -> 54.6 us
  blocking collectives: 37.9 us -> 43.7 us
  Pallas kernels: 13 us -> 10.6 us
    all_to_all x1, starting transfers between devices: 19.2 us -> 9.83 us  [local(): coeffs = lax.all_to_all(coeffs, GROUP, 0, 0, tiled=True)]
    ppermute x1, waiting for transfers between devices: 10.3 us -> 17.5 us  [local(): other = lax.ppermute(spectra, ('yh',), [(0, 1), (1, 0)])]
    all_to_all x1, blocking collectives: 26.2 us -> 32 us  [local(): back = lax.all_to_all(back, GROUP, 0, 0, tiled=True)]
    all_to_all x1, starting transfers between devices: 10 us -> 4.79 us  [local(): lax.all_to_all(rows_out.reshape(8, HALF, -1), ('z',), 0, 0, tiled=True)]
    all_to_all x1, waiting for transfers between devices: 17.5 us -> 22.2 us  [local(): lax.all_to_all(rows_out.reshape(8, HALF, -1), ('z',), 0, 0, tiled=True)]
    all_to_all x1, waiting for transfers between devices: 12.2 us -> 9.18 us  [local(): coeffs = lax.all_to_all(coeffs, GROUP, 0, 0, tiled=True)]
    ppermute x1, starting transfers between devices: 5.28 us -> 2.39 us  [local(): far = lax.ppermute(near, ('c',), [(0, 1), (1, 0)])]
    ppermute x1, starting transfers between devices: 2.72 us -> 5.18 us  [local(): other = lax.ppermute(spectra, ('yh',), [(0, 1), (1, 0)])]
where the time goes in v4:
time: 145 us
  waiting for transfers between devices  54.6 us (38%)
  blocking collectives  43.7 us (30%)
  starting transfers between devices  27.8 us (19%)
  Pallas kernels  10.6 us (7%)
  local copies, waits for them, and re-layouts  7.06 us (5%)
    all_to_all x1, blocking collectives, local(): back = lax.all_to_all(back, GROUP, 0, 0, tiled=True)  32 us
    all_to_all x1, waiting for transfers between devices, local(): lax.all_to_all(rows_out.reshape(8, HALF, -1), ('z',), 0, 0, tiled=True)  22.2 us
    ppermute x1, waiting for transfers between devices, local(): other = lax.ppermute(spectra, ('yh',), [(0, 1), (1, 0)])  17.5 us
    all_to_all x1, blocking collectives, local(): rows_out = lax.all_to_all(rows_out, ('c',), 0, 0, tiled=True)  11.7 us
    pallas_call x8, Pallas kernels, call(): pl.pallas_call(kernel, out_shape=out_shapes, in_specs=[smem if i < scalar...  10.6 us
    all_to_all x1, starting transfers between devices, local(): coeffs = lax.all_to_all(coeffs, GROUP, 0, 0, tiled=True)  9.83 us
    all_to_all x1, waiting for transfers between devices, local(): coeffs = lax.all_to_all(coeffs, GROUP, 0, 0, tiled=True)  9.18 us
    unnamed x30, local copies, waits for them, and re-layouts  6.65 us
  transfers between devices with their start and end apart: 5, of which 4 were waited for; matrix products, arithmetic and copies ran while one was open for 0% of the time, Pallas kernels for 4%

profile of v4, /device:TPU:1, one launch (start us, length us, event | category | flops | bytes accessed | tf_op | source)
XLA Modules:
  0.0 144.7 jit_solution(1891258702663743234)
XLA Ops:
  0.6 0.0 copy-start.7
  0.6 1.0 copy-done.7
  1.6 0.0 copy-start.8
  1.6 1.0 copy-done.8
  2.6 0.1 shard_map.97
  2.7 0.0 copy-start.12
  2.8 0.0 copy-start.13
  2.8 11.7 %all_to_all.25 = f32[2,4,24,1152]{3,2,1,0:T(8,128)} all-to-all(f32[2,4,24,1152]{3,2,1,0:T(8,128)S(1)} %shard_map.97), channel_id=1, replica_groups=mesh['yh'=2,'z'=8,'yl'=4,'x'=4,'c'=2] {'c'}, dimensions={0} | all-to-all | bytes 1769472 | tf_op jit(solution)/shard_map/all_to_all | solution.py:223
  14.5 4.8 %all-to-all-start.1 = ((f32[8,24,1152]{2,1,0:T(8,128)}), f32[8,24,1152]{2,1,0:T(8,128)S(1)}, u32[]{:S(2)}, u32[]{:S(2)}) async-start(f32[8,24,1152]{2,1,0:T(8,128)} %bitcast.4), calls=%async_computation.1 | async-start | bytes 1769472 | tf_op jit(solution)/shard_map/all_to_all | solution.py:224
  19.3 0.0 copy-done.12
  19.3 0.0 copy-done.13
  19.3 0.0 copy-start.5
  19.3 0.0 copy-start.6
  19.3 1.3 copy-done.6
  20.6 0.4 shard_map.96.w_ref
  21.1 0.0 copy-done
  21.1 0.0 copy-done.1
  21.1 0.0 copy-done.5
  21.1 1.7 %shard_map.95 = f32[128,4,128]{2,1,0:T(4,128)} custom-call(f32[5,45,1440]{2,1,0:T(8,128)S(1)} %copy-done.5, bf16[256,1440]{1,0:T(8,128)(2,1)S(1)} %copy-done, bf16[256,1440]{1,0:T(8,128)(2,1)S(1)} %copy-done.1), custom_call_target="tpu_custom_call" | custom-call | flops 600000000 | bytes 3032704 | tf_op jit(solution)/shard_map/pallas_call | solution.py:190
  22.8 22.2 %all-to-all-done.1.near_ref = f32[8,24,1152]{2,1,0:T(8,128)S(1)} async-done(((f32[8,24,1152]{2,1,0:T(8,128)}), f32[8,24,1152]{2,1,0:T(8,128)S(1)}, u32[]{:S(2)}, u32[]{:S(2)}) %all-to-all-start.1) | async-done | bytes 884768 | tf_op jit(solution)/shard_map/all_to_all | solution.py:224
  45.0 2.4 %collective-permute-start = (f32[8,24,1152]{2,1,0:T(8,128)S(1)}, f32[8,24,1152]{2,1,0:T(8,128)}, u32[]{:S(2)}, u32[]{:S(2)}) collective-permute-start(f32[8,24,1152]{2,1,0:T(8,128)S(1)} %all-to-all-done.1.near_ref), channel_id=1, source_target_pairs={{0,1},{1,0},{2,3},{3,2},{4,5},{5,4},{6,7},{7,6},{8,9},{9,8},{10,11... | collective-permute-start | bytes 2654216 | tf_op jit(solution)/shard_map/ppermute | solution.py:235
  47.4 9.8 %all-to-all-start.2 = ((f32[128,4,128]{2,1,0:T(4,128)}), f32[128,4,128]{2,1,0:T(4,128)}, u32[]{:S(2)}, u32[]{:S(2)}) async-start(f32[128,4,128]{2,1,0:T(4,128)} %shard_map.95), calls=%async_computation.2 | async-start | bytes 524288 | tf_op jit(solution)/shard_map/all_to_all | solution.py:236
  57.2 0.1 pad_add_fusion.place_ref
  57.3 0.0 collective-permute-done.far_ref
  57.3 2.2 %shard_map.98 = (bf16[384,720]{1,0:T(8,128)(2,1)S(1)}, bf16[384,720]{1,0:T(8,128)(2,1)S(1)}, f32[160,360]{1,0:T(8,128)S(1)}) custom-call(s32[3]{0:T(128)S(1)} %pad_add_fusion.place_ref, s32[1,80]{1,0:T(1,128)S(1)} %broadcast_select_fusion.slots_ref, f32[8,24,1152]{2,1,0:T(8,128)S(1)} %all-to-all-done.1.near_ref, f32[8,24,1152]{2,1,0:T(8,128)} %collective-permute-done.far_ref), custom_call_target="tpu_custom_call" | custom-call | flops 100000000 | bytes 3106124 | tf_op jit(solution)/shard_map/pallas_call | solution.py:190
  59.5 0.0 copy-start.2
  59.5 0.8 copy-done.2
  60.4 0.7 copy-done.9
  61.0 9.2 %all-to-all-done.2.x_ref = f32[128,4,128]{2,1,0:T(4,128)} async-done(((f32[128,4,128]{2,1,0:T(4,128)}), f32[128,4,128]{2,1,0:T(4,128)}, u32[]{:S(2)}, u32[]{:S(2)}) %all-to-all-start.2) | async-done | bytes 262176 | tf_op jit(solution)/shard_map/all_to_all | solution.py:236
  70.2 1.1 copy-done.3
  71.3 1.8 %shard_map.99.near_ref = f32[160,720]{1,0:T(8,128)S(1)} custom-call(f32[128,4,128]{2,1,0:T(4,128)} %all-to-all-done.2.x_ref, bf16[384,720]{1,0:T(8,128)(2,1)S(1)} %get-tuple-element.10.lh_ref, bf16[384,720]{1,0:T(8,128)(2,1)S(1)} %copy-done.3), custom_call_target="tpu_custom_call" | custom-call | flops 300000000 | bytes 1828864 | tf_op jit(solution)/shard_map/pallas_call | solution.py:190
  73.1 5.2 %collective-permute-start.1 = (f32[160,720]{1,0:T(8,128)S(1)}, f32[160,720]{1,0:T(8,128)S(1)}, u32[]{:S(2)}, u32[]{:S(2)}) collective-permute-start(f32[160,720]{1,0:T(8,128)S(1)} %shard_map.99.near_ref), channel_id=1, source_target_pairs={{0,256},{256,0},{1,257},{257,1},{2,258},{258,2},{3,259},{259,3},{4... | collective-permute-start | bytes 1382408 | tf_op jit(solution)/shard_map/ppermute | solution.py:256
  78.3 17.5 %collective-permute-done.1.far_ref = f32[160,720]{1,0:T(8,128)S(1)} collective-permute-done((f32[160,720]{1,0:T(8,128)S(1)}, f32[160,720]{1,0:T(8,128)S(1)}, u32[]{:S(2)}, u32[]{:S(2)}) %collective-permute-start.1) | collective-permute-done | bytes 460832 | tf_op jit(solution)/shard_map/ppermute | solution.py:256
  95.8 0.0 copy-done.4
  95.8 0.0 copy-done.10
  95.8 1.6 %shard_map.100 = f32[128,8,128]{2,1,0:T(8,128)S(1)} custom-call(s32[3]{0:T(128)S(1)} %pad_add_fusion.place_ref, f32[160,720]{1,0:T(8,128)S(1)} %shard_map.99.near_ref, f32[160,720]{1,0:T(8,128)S(1)} %collective-permute-done.1.far_ref, bf16[384,720]{1,0:T(8,128)(2,1)S(1)} %get-tuple-element.10.lh_ref, bf16[384,720]{1,0:T(8,128)(2,1)S(1)} %copy-done.4, ...), custom_call_target="tpu_custom_call" | custom-call | flops 300000000 | bytes 3243020 | tf_op jit(solution)/shard_map/pallas_call | solution.py:190
  97.4 0.0 copy-start.11
  97.4 32.0 %all_to_all.26.x_ref = f32[128,8,128]{2,1,0:T(8,128)S(1)} all-to-all(f32[128,8,128]{2,1,0:T(8,128)S(1)} %shard_map.100), channel_id=1, replica_groups=mesh['yh'=2,'z'=8,'yl'=4,'x'=4,'c'=2] {'z','yl','x'}, dimensions={0} | all-to-all | bytes 1048576 | tf_op jit(solution)/shard_map/all_to_all | solution.py:265
  129.4 0.8 shard_map.102
  130.2 5.6 %all-to-all-start.4 = ((f32[32,4,128]{2,1,0:T(4,128)}), f32[32,4,128]{2,1,0:T(4,128)S(1)}, u32[]{:S(2)}, u32[]{:S(2)}) async-start(f32[32,4,128]{2,1,0:T(4,128)} %shard_map.102), calls=%async_computation.4 | async-start | bytes 131072 | tf_op jit(solution)/shard_map/all_to_all | solution.py:268
  135.8 0.0 copy-done.11
  135.8 0.1 copy.12.lw_ref
  135.9 2.0 %shard_map.101 = f32[5,45,1440]{2,1,0:T(8,128)} custom-call(f32[128,8,128]{2,1,0:T(8,128)S(1)} %all_to_all.26.x_ref, bf16[256,1440]{1,0:T(8,128)(2,1)S(1)} %copy-done, bf16[256,1440]{1,0:T(8,128)(2,1)S(1)} %copy-done.1, f32[45,1]{1,0:T(8,128)S(1)} %copy.12.lw_ref), custom_call_target="tpu_custom_call" | custom-call | flops 600000000 | bytes 3295028 | tf_op jit(solution)/shard_map/pallas_call | solution.py:190
  137.9 5.7 %all-to-all-done.4 = f32[32,4,128]{2,1,0:T(4,128)S(1)} async-done(((f32[32,4,128]{2,1,0:T(4,128)}), f32[32,4,128]{2,1,0:T(4,128)S(1)}, u32[]{:S(2)}, u32[]{:S(2)}) %all-to-all-start.4) | async-done | bytes 65568 | tf_op jit(solution)/shard_map/all_to_all | solution.py:268
  143.6 0.1 reshape.21
  143.7 0.1 reshape.22
  143.8 0.1 copy.14
  144.0 0.8 copy.15
  (9 shorter events, 0.0 us)
Async XLA Ops:
  0.6 1.0 copy-start.7
  1.6 1.0 copy-start.8
  2.7 16.5 %copy-start.12 = (s32[1,80]{1,0:T(1,128)S(1)}, s32[1,80]{1,0:T(1,128)}, u32[]{:S(2)}) copy-start(s32[1,80]{1,0:T(1,128)} %constant.35) | copy-start | bytes 964
  2.8 16.5 %copy-start.13 = (s32[1,80]{1,0:T(1,128)S(1)}, s32[1,80]{1,0:T(1,128)}, u32[]{:S(2)}) copy-start(s32[1,80]{1,0:T(1,128)} %constant.36) | copy-start | bytes 964
  14.5 6.6 %copy-start = (bf16[256,1440]{1,0:T(8,128)(2,1)S(1)}, bf16[256,1440]{1,0:T(8,128)(2,1)}, u32[]{:S(2)}) copy-start(bf16[256,1440]{1,0:T(8,128)(2,1)} %constant.29.clone.th_ref) | copy-start | bytes 2211844
  14.5 6.6 %copy-start.1 = (bf16[256,1440]{1,0:T(8,128)(2,1)S(1)}, bf16[256,1440]{1,0:T(8,128)(2,1)}, u32[]{:S(2)}) copy-start(bf16[256,1440]{1,0:T(8,128)(2,1)} %constant.30.clone.tl_ref) | copy-start | bytes 2211844
  14.5 30.5 %all-to-all-start.1 = ((f32[8,24,1152]{2,1,0:T(8,128)}), f32[8,24,1152]{2,1,0:T(8,128)S(1)}, u32[]{:S(2)}, u32[]{:S(2)}) async-start(f32[8,24,1152]{2,1,0:T(8,128)} %bitcast.4), calls=%async_computation.1 | async-start | bytes 1769472 | tf_op jit(solution)/shard_map/all_to_all | solution.py:224
  19.3 1.8 %copy-start.5 = (f32[5,45,1440]{2,1,0:T(8,128)S(1)}, f32[5,45,1440]{2,1,0:T(8,128)}, u32[]{:S(2)}) copy-start(f32[5,45,1440]{2,1,0:T(8,128)} %g_ref.1) | copy-start | bytes 3888004
  19.3 1.3 copy-start.6
  45.0 12.3 %collective-permute-start = (f32[8,24,1152]{2,1,0:T(8,128)S(1)}, f32[8,24,1152]{2,1,0:T(8,128)}, u32[]{:S(2)}, u32[]{:S(2)}) collective-permute-start(f32[8,24,1152]{2,1,0:T(8,128)S(1)} %all-to-all-done.1.near_ref), channel_id=1, source_target_pairs={{0,1},{1,0},{2,3},{3,2},{4,5},{5,4},{6,7},{7,6},{8,9},{9,8},{10,11... | collective-permute-start | bytes 2654216 | tf_op jit(solution)/shard_map/ppermute | solution.py:235
  47.4 22.9 %all-to-all-start.2 = ((f32[128,4,128]{2,1,0:T(4,128)}), f32[128,4,128]{2,1,0:T(4,128)}, u32[]{:S(2)}, u32[]{:S(2)}) async-start(f32[128,4,128]{2,1,0:T(4,128)} %shard_map.95), calls=%async_computation.2 | async-start | bytes 524288 | tf_op jit(solution)/shard_map/all_to_all | solution.py:236
  59.5 0.8 copy-start.2
  60.4 0.7 copy-start.9
  70.2 1.1 copy-start.3
  71.3 24.5 %copy-start.4 = (bf16[384,720]{1,0:T(8,128)(2,1)S(1)}, bf16[384,720]{1,0:T(8,128)(2,1)}, u32[]{:S(2)}) copy-start(bf16[384,720]{1,0:T(8,128)(2,1)} %copy-done.2) | copy-start | bytes 1658884
  71.3 24.5 %copy-start.10 = (f32[160,360]{1,0:T(8,128)S(1)}, f32[160,360]{1,0:T(8,128)}, u32[]{:S(2)}) copy-start(f32[160,360]{1,0:T(8,128)} %copy-done.9) | copy-start | bytes 691204
  73.1 22.7 %collective-permute-start.1 = (f32[160,720]{1,0:T(8,128)S(1)}, f32[160,720]{1,0:T(8,128)S(1)}, u32[]{:S(2)}, u32[]{:S(2)}) collective-permute-start(f32[160,720]{1,0:T(8,128)S(1)} %shard_map.99.near_ref), channel_id=1, source_target_pairs={{0,256},{256,0},{1,257},{257,1},{2,258},{258,2},{3,259},{259,3},{4... | collective-permute-start | bytes 1382408 | tf_op jit(solution)/shard_map/ppermute | solution.py:256
  97.4 38.4 %copy-start.11 = (f32[45]{0:T(128)S(1)}, f32[45]{0:T(128)}, u32[]{:S(2)}) copy-start(f32[45]{0:T(128)} %param.12) | copy-start | bytes 544
  130.2 13.4 %all-to-all-start.4 = ((f32[32,4,128]{2,1,0:T(4,128)}), f32[32,4,128]{2,1,0:T(4,128)S(1)}, u32[]{:S(2)}, u32[]{:S(2)}) async-start(f32[32,4,128]{2,1,0:T(4,128)} %shard_map.102), calls=%async_computation.4 | async-start | bytes 131072 | tf_op jit(solution)/shard_map/all_to_all | solution.py:268

commit v5 on v4

--- a/solution.py
+++ b/solution.py
@@ -19,7 +19,7 @@
 F32 = jnp.float32
 WIDE = 48
 HALF = WIDE // 2
-SAVED = 768
+TOP = HALF - 1
 PICK = (((0,), (1,)), ((), ()))
 NN = (((1,), (0,)), ((), ()))
 NT = (((1,), (1,)), ((), ()))
@@ -64,15 +64,19 @@
 def prepare_kernel(leg_ref, saved_ref, out_ref):
     orders, rows, degrees = leg_ref.shape
     channels = saved_ref.shape[3]
+    lanes = out_ref.shape[3]
+    fit = lanes - degrees - channels
+    rest = channels - fit
     out_ref[...] = jnp.zeros_like(out_ref)
-    for side in range(2):
-        n = min(HALF, rows - side * HALF)
-        at = slice(side * HALF, side * HALF + n)
+    for side, (low, n) in enumerate(((0, TOP), (TOP, rows - TOP))):
+        at = slice(low, low + n)
         for k in range(orders):
             out_ref[side, k, :n, :degrees] = leg_ref[k, at, :]
-            for r in range(2):
-                lane = SAVED + r * channels
-                out_ref[side, k, :n, lane : lane + channels] = saved_ref[at, k, r, :]
+            out_ref[side, k, :n, degrees : degrees + channels] = saved_ref[at, k, 0, :]
+            out_ref[side, k, :n, degrees + channels :] = saved_ref[at, k, 1, :fit]
+            for i in range(n):
+                tail = saved_ref[low + i : low + i + 1, k, 1, fit:]
+                out_ref[side, k, TOP:HALF, i * rest : (i + 1) * rest] = tail
 
 
 def picks(slots_ref, channels):
@@ -92,7 +96,8 @@
     group, rows, points = g_ref.shape
     field[...] = jnp.zeros_like(field)
     for j in range(group):
-        field[j * WIDE : j * WIDE + rows, :] = g_ref[j]
+        field[j * WIDE : j * WIDE + TOP, :] = g_ref[j, :TOP, :]
+        field[j * WIDE + HALF : j * WIDE + HALF + rows - TOP, :] = g_ref[j, TOP:, :]
     high, low = two(field[...])
     table = th_ref[...]
     acc = dot(table, high, NT) + dot(table, low, NT) + dot(tl_ref[...], high, NT)
@@ -101,24 +106,32 @@
             out_ref[:, 2 * r + k, :] = acc[r * 128 : (r + 1) * 128, k * 128 : (k + 1) * 128]
 
 
-def split_kernel(place_ref, slots_ref, near_ref, far_ref, lh_ref, ll_ref, sv_ref, both):
+def split_kernel(place_ref, slots_ref, near_ref, far_ref, lh_ref, ll_ref, sv_ref, both, second):
     degrees = lh_ref.shape[1]
     half = sv_ref.shape[0] // 2
     channels = 2 * half
     rows = degrees // 16
+    fit = both.shape[2] - degrees - channels
+    rest = channels - fit
     c = place_ref[0]
     both[:, pl.ds(pl.multiple_of(c * HALF, HALF), HALF), :] = near_ref[...]
     both[:, pl.ds(pl.multiple_of((1 - c) * HALF, HALF), HALF), :] = far_ref[...]
     high, low = two(both[:, :, :degrees].reshape(8 * WIDE, degrees))
     lh_ref[...] = high
     ll_ref[...] = low
+    second[...] = jnp.zeros_like(second)
+    second[:, :, :fit] = both[:, :, degrees + channels :]
+    for side, n in enumerate((TOP, rows - TOP)):
+        for i in range(n):
+            second[:, side * HALF + i, fit:] = both[:, side * HALF + TOP, i * rest : (i + 1) * rest]
     pick = picks(slots_ref, channels)
-    for r in range(2):
-        lane = SAVED + r * channels
-        v = both[:, :, lane : lane + channels].reshape(8 * WIDE, channels)
-        mine = sum(dot(pick, term, PICK) for term in three(v))
+    for r, v in enumerate((both[:, :, degrees : degrees + channels], second[...])):
+        mine = sum(dot(pick, term, PICK) for term in three(v.reshape(8 * WIDE, channels)))
+        to = slice(r * half, (r + 1) * half)
         for a in range(8):
-            sv_ref[r * half : (r + 1) * half, a * rows : (a + 1) * rows] = mine[:, a * WIDE : a * WIDE + rows]
+            at, src = a * rows, a * WIDE
+            sv_ref[to, at : at + TOP] = mine[:, src : src + TOP]
+            sv_ref[to, at + TOP : at + rows] = mine[:, src + HALF : src + HALF + rows - TOP]
 
 
 def analysis_kernel(x_ref, lh_ref, ll_ref, out_ref, ct, tmp):
@@ -179,7 +192,9 @@
     table = th_ref[...]
     acc = dot(high, table, TN) + dot(low, table, TN) + dot(high, tl_ref[...], TN)
     for j in range(group):
-        out_ref[j] = acc[j * WIDE : j * WIDE + rows] * lw_ref[...]
+        at = j * WIDE
+        out_ref[j, :TOP, :] = acc[at : at + TOP] * lw_ref[:TOP, :]
+        out_ref[j, TOP:, :] = acc[at + HALF : at + HALF + rows - TOP] * lw_ref[TOP:, :]
 
 
 def call(kernel, args, out_shapes, flops, scratch=(), scalars=0, hbm_out=False):
@@ -217,7 +232,7 @@
     rows_out = call(
         prepare_kernel,
         (legendre, saved_spectra),
-        shape(2, orders + 1, HALF, SAVED + 3 * 128),
+        shape(2, orders + 1, HALF, 8 * 128),
         1000,
     )
     rows_out = lax.all_to_all(rows_out, ("c",), 0, 0, tiled=True)
@@ -243,7 +258,7 @@
             shape(2 * half, degrees // 2),
         ),
         100_000_000,
-        scratch=[pltpu.VMEM((8, WIDE, SAVED + 3 * 128), F32)],
+        scratch=[pltpu.VMEM((8, WIDE, 8 * 128), F32), pltpu.VMEM((8, WIDE, channels), F32)],
         scalars=1,
     )
     spectra = call(

time: 145 us -> 143 us (0.986)
  waiting for transfers between devices: 54.6 us -> 51.7 us
    all_to_all x1, waiting for transfers between devices: 22.2 us -> 20 us  [local(): lax.all_to_all(rows_out.reshape(8, HALF, -1), ('z',), 0, 0, tiled=True)]
    unnamed x30 -> x28, local copies, waits for them, and re-layouts: 6.65 us -> 6.65 us
  transfers between devices with their start and end apart: 5 -> 5, of which waited for: 4 -> 4; matrix products, arithmetic and copies ran while one was open for 0% -> 0% of each run, Pallas kernels for 4% -> 5%
where the time goes in v5:
time: 143 us
  waiting for transfers between devices  51.7 us (36%)
  blocking collectives  43.7 us (31%)
  starting transfers between devices  27.8 us (19%)
  Pallas kernels  11.4 us (8%)
  local copies, waits for them, and re-layouts  7.06 us (5%)
    all_to_all x1, blocking collectives, local(): back = lax.all_to_all(back, GROUP, 0, 0, tiled=True)  32 us
    all_to_all x1, waiting for transfers between devices, local(): lax.all_to_all(rows_out.reshape(8, HALF, -1), ('z',), 0, 0, tiled=True)  20 us
    ppermute x1, waiting for transfers between devices, local(): other = lax.ppermute(spectra, ('yh',), [(0, 1), (1, 0)])  17.4 us
    all_to_all x1, blocking collectives, local(): rows_out = lax.all_to_all(rows_out, ('c',), 0, 0, tiled=True)  11.6 us
    pallas_call x8, Pallas kernels, call(): pl.pallas_call(kernel, out_shape=out_shapes, in_specs=[smem if i < scalar...  11.4 us
    all_to_all x1, starting transfers between devices, local(): coeffs = lax.all_to_all(coeffs, GROUP, 0, 0, tiled=True)  9.83 us
    all_to_all x1, waiting for transfers between devices, local(): coeffs = lax.all_to_all(coeffs, GROUP, 0, 0, tiled=True)  8.56 us
    unnamed x28, local copies, waits for them, and re-layouts  6.65 us
  transfers between devices with their start and end apart: 5, of which 4 were waited for; matrix products, arithmetic and copies ran while one was open for 0% of the time, Pallas kernels for 5%

profile of v5, /device:TPU:1, one launch (start us, length us, event | category | flops | bytes accessed | tf_op | source)
XLA Modules:
  0.0 142.6 jit_solution(12768534054659684599)
XLA Ops:
  0.6 0.0 copy-start.6
  0.6 1.0 copy-done.6
  1.6 0.0 copy-start.7
  1.6 1.0 copy-done.7
  2.6 0.3 shard_map.97
  2.9 0.0 copy-start.11
  2.9 0.0 copy-start.12
  2.9 11.6 %all_to_all.25 = f32[2,4,24,1024]{3,2,1,0:T(8,128)} all-to-all(f32[2,4,24,1024]{3,2,1,0:T(8,128)S(1)} %shard_map.97), channel_id=1, replica_groups=mesh['yh'=2,'z'=8,'yl'=4,'x'=4,'c'=2] {'c'}, dimensions={0} | all-to-all | bytes 1572864 | tf_op jit(solution)/shard_map/all_to_all | solution.py:238
  14.6 0.0 copy-start
  14.6 4.8 %all-to-all-start.1 = ((f32[8,24,1024]{2,1,0:T(8,128)}), f32[8,24,1024]{2,1,0:T(8,128)S(1)}, u32[]{:S(2)}, u32[]{:S(2)}) async-start(f32[8,24,1024]{2,1,0:T(8,128)} %bitcast.13), calls=%async_computation.1 | async-start | bytes 1572864 | tf_op jit(solution)/shard_map/all_to_all | solution.py:239
  19.4 0.0 copy-done.11
  19.4 0.0 copy-done.12
  19.4 0.0 copy-start.4
  19.4 0.0 copy-start.5
  19.4 1.3 copy-done.5
  20.7 0.5 shard_map.96.w_ref
  21.2 0.0 copy-done
  21.2 0.0 copy-done.1
  21.2 0.0 copy-done.4
  21.2 1.7 %shard_map.95 = f32[128,4,128]{2,1,0:T(4,128)} custom-call(f32[5,45,1440]{2,1,0:T(8,128)S(1)} %copy-done.4, bf16[256,1440]{1,0:T(8,128)(2,1)S(1)} %copy-done, bf16[256,1440]{1,0:T(8,128)(2,1)S(1)} %copy-done.1), custom_call_target="tpu_custom_call" | custom-call | flops 600000000 | bytes 3032704 | tf_op jit(solution)/shard_map/pallas_call | solution.py:205
  22.9 20.0 %all-to-all-done.1.near_ref = f32[8,24,1024]{2,1,0:T(8,128)S(1)} async-done(((f32[8,24,1024]{2,1,0:T(8,128)}), f32[8,24,1024]{2,1,0:T(8,128)S(1)}, u32[]{:S(2)}, u32[]{:S(2)}) %all-to-all-start.1) | async-done | bytes 786464 | tf_op jit(solution)/shard_map/all_to_all | solution.py:239
  42.9 2.4 %collective-permute-start = (f32[8,24,1024]{2,1,0:T(8,128)S(1)}, f32[8,24,1024]{2,1,0:T(8,128)}, u32[]{:S(2)}, u32[]{:S(2)}) collective-permute-start(f32[8,24,1024]{2,1,0:T(8,128)S(1)} %all-to-all-done.1.near_ref), channel_id=1, source_target_pairs={{0,1},{1,0},{2,3},{3,2},{4,5},{5,4},{6,7},{7,6},{8,9},{9,8},{10,11... | collective-permute-start | bytes 2359304 | tf_op jit(solution)/shard_map/ppermute | solution.py:250
  45.3 9.8 %all-to-all-start.2 = ((f32[128,4,128]{2,1,0:T(4,128)}), f32[128,4,128]{2,1,0:T(4,128)}, u32[]{:S(2)}, u32[]{:S(2)}) async-start(f32[128,4,128]{2,1,0:T(4,128)} %shard_map.95), calls=%async_computation.2 | async-start | bytes 524288 | tf_op jit(solution)/shard_map/all_to_all | solution.py:251
  55.2 0.1 pad_add_fusion.place_ref
  55.3 0.0 collective-permute-done.far_ref
  55.3 2.8 %shard_map.98 = (bf16[384,720]{1,0:T(8,128)(2,1)S(1)}, bf16[384,720]{1,0:T(8,128)(2,1)S(1)}, f32[160,360]{1,0:T(8,128)S(1)}) custom-call(s32[3]{0:T(128)S(1)} %pad_add_fusion.place_ref, s32[1,80]{1,0:T(1,128)S(1)} %broadcast_select_fusion.slots_ref, f32[8,24,1024]{2,1,0:T(8,128)S(1)} %all-to-all-done.1.near_ref, f32[8,24,1024]{2,1,0:T(8,128)} %collective-permute-done.far_ref), custom_call_target="tpu_custom_call" | custom-call | flops 100000000 | bytes 2909516 | tf_op jit(solution)/shard_map/pallas_call | solution.py:205
  58.1 0.0 copy-start.2
  58.1 0.8 copy-done.2
  58.9 0.7 copy-done.8
  59.6 8.6 %all-to-all-done.2.x_ref = f32[128,4,128]{2,1,0:T(4,128)} async-done(((f32[128,4,128]{2,1,0:T(4,128)}), f32[128,4,128]{2,1,0:T(4,128)}, u32[]{:S(2)}, u32[]{:S(2)}) %all-to-all-start.2) | async-done | bytes 262176 | tf_op jit(solution)/shard_map/all_to_all | solution.py:251
  68.2 1.1 copy-done.3
  69.2 1.8 %shard_map.99.near_ref = f32[160,720]{1,0:T(8,128)S(1)} custom-call(f32[128,4,128]{2,1,0:T(4,128)} %all-to-all-done.2.x_ref, bf16[384,720]{1,0:T(8,128)(2,1)S(1)} %get-tuple-element.10.lh_ref, bf16[384,720]{1,0:T(8,128)(2,1)S(1)} %copy-done.3), custom_call_target="tpu_custom_call" | custom-call | flops 300000000 | bytes 1828864 | tf_op jit(solution)/shard_map/pallas_call | solution.py:205
  71.0 5.2 %collective-permute-start.1 = (f32[160,720]{1,0:T(8,128)S(1)}, f32[160,720]{1,0:T(8,128)S(1)}, u32[]{:S(2)}, u32[]{:S(2)}) collective-permute-start(f32[160,720]{1,0:T(8,128)S(1)} %shard_map.99.near_ref), channel_id=1, source_target_pairs={{0,256},{256,0},{1,257},{257,1},{2,258},{258,2},{3,259},{259,3},{4... | collective-permute-start | bytes 1382408 | tf_op jit(solution)/shard_map/ppermute | solution.py:271
  76.2 17.4 %collective-permute-done.1.far_ref = f32[160,720]{1,0:T(8,128)S(1)} collective-permute-done((f32[160,720]{1,0:T(8,128)S(1)}, f32[160,720]{1,0:T(8,128)S(1)}, u32[]{:S(2)}, u32[]{:S(2)}) %collective-permute-start.1) | collective-permute-done | bytes 460832 | tf_op jit(solution)/shard_map/ppermute | solution.py:271
  93.7 0.0 copy-done.9
  93.7 1.6 %shard_map.100 = f32[128,8,128]{2,1,0:T(8,128)S(1)} custom-call(s32[3]{0:T(128)S(1)} %pad_add_fusion.place_ref, f32[160,720]{1,0:T(8,128)S(1)} %shard_map.99.near_ref, f32[160,720]{1,0:T(8,128)S(1)} %collective-permute-done.1.far_ref, bf16[384,720]{1,0:T(8,128)(2,1)S(1)} %get-tuple-element.10.lh_ref, bf16[384,720]{1,0:T(8,128)(2,1)S(1)} %copy-done.3, ...), custom_call_target="tpu_custom_call" | custom-call | flops 300000000 | bytes 3243020 | tf_op jit(solution)/shard_map/pallas_call | solution.py:205
  95.2 0.0 copy-start.10
  95.3 32.0 %all_to_all.26.x_ref = f32[128,8,128]{2,1,0:T(8,128)S(1)} all-to-all(f32[128,8,128]{2,1,0:T(8,128)S(1)} %shard_map.100), channel_id=1, replica_groups=mesh['yh'=2,'z'=8,'yl'=4,'x'=4,'c'=2] {'z','yl','x'}, dimensions={0} | all-to-all | bytes 1048576 | tf_op jit(solution)/shard_map/all_to_all | solution.py:280
  127.3 0.8 shard_map.102
  128.1 5.6 %all-to-all-start.4 = ((f32[32,4,128]{2,1,0:T(4,128)}), f32[32,4,128]{2,1,0:T(4,128)S(1)}, u32[]{:S(2)}, u32[]{:S(2)}) async-start(f32[32,4,128]{2,1,0:T(4,128)} %shard_map.102), calls=%async_computation.4 | async-start | bytes 131072 | tf_op jit(solution)/shard_map/all_to_all | solution.py:283
  133.7 0.0 copy-done.10
  133.7 0.1 copy.12.lw_ref
  133.8 2.0 %shard_map.101 = f32[5,45,1440]{2,1,0:T(8,128)} custom-call(f32[128,8,128]{2,1,0:T(8,128)S(1)} %all_to_all.26.x_ref, bf16[256,1440]{1,0:T(8,128)(2,1)S(1)} %copy-done, bf16[256,1440]{1,0:T(8,128)(2,1)S(1)} %copy-done.1, f32[45,1]{1,0:T(8,128)S(1)} %copy.12.lw_ref), custom_call_target="tpu_custom_call" | custom-call | flops 600000000 | bytes 3295028 | tf_op jit(solution)/shard_map/pallas_call | solution.py:205
  135.8 5.7 %all-to-all-done.4 = f32[32,4,128]{2,1,0:T(4,128)S(1)} async-done(((f32[32,4,128]{2,1,0:T(4,128)}), f32[32,4,128]{2,1,0:T(4,128)S(1)}, u32[]{:S(2)}, u32[]{:S(2)}) %all-to-all-start.4) | async-done | bytes 65568 | tf_op jit(solution)/shard_map/all_to_all | solution.py:283
  141.5 0.1 reshape.21
  141.6 0.1 reshape.22
  141.7 0.1 copy.14
  141.9 0.8 copy.15
  (7 shorter events, 0.0 us)
Async XLA Ops:
  0.6 1.0 copy-start.6
  1.6 1.0 copy-start.7
  2.9 16.5 %copy-start.11 = (s32[1,80]{1,0:T(1,128)S(1)}, s32[1,80]{1,0:T(1,128)}, u32[]{:S(2)}) copy-start(s32[1,80]{1,0:T(1,128)} %constant.35) | copy-start | bytes 964
  2.9 16.5 %copy-start.12 = (s32[1,80]{1,0:T(1,128)S(1)}, s32[1,80]{1,0:T(1,128)}, u32[]{:S(2)}) copy-start(s32[1,80]{1,0:T(1,128)} %constant.36) | copy-start | bytes 964
  14.6 6.6 %copy-start = (bf16[256,1440]{1,0:T(8,128)(2,1)S(1)}, bf16[256,1440]{1,0:T(8,128)(2,1)}, u32[]{:S(2)}) copy-start(bf16[256,1440]{1,0:T(8,128)(2,1)} %constant.29.clone.th_ref) | copy-start | bytes 2211844
  14.6 6.6 %copy-start.1 = (bf16[256,1440]{1,0:T(8,128)(2,1)S(1)}, bf16[256,1440]{1,0:T(8,128)(2,1)}, u32[]{:S(2)}) copy-start(bf16[256,1440]{1,0:T(8,128)(2,1)} %constant.30.clone.tl_ref) | copy-start | bytes 2211844
  14.6 28.4 %all-to-all-start.1 = ((f32[8,24,1024]{2,1,0:T(8,128)}), f32[8,24,1024]{2,1,0:T(8,128)S(1)}, u32[]{:S(2)}, u32[]{:S(2)}) async-start(f32[8,24,1024]{2,1,0:T(8,128)} %bitcast.13), calls=%async_computation.1 | async-start | bytes 1572864 | tf_op jit(solution)/shard_map/all_to_all | solution.py:239
  19.4 1.8 %copy-start.4 = (f32[5,45,1440]{2,1,0:T(8,128)S(1)}, f32[5,45,1440]{2,1,0:T(8,128)}, u32[]{:S(2)}) copy-start(f32[5,45,1440]{2,1,0:T(8,128)} %g_ref.1) | copy-start | bytes 3888004
  19.4 1.3 copy-start.5
  42.9 12.3 %collective-permute-start = (f32[8,24,1024]{2,1,0:T(8,128)S(1)}, f32[8,24,1024]{2,1,0:T(8,128)}, u32[]{:S(2)}, u32[]{:S(2)}) collective-permute-start(f32[8,24,1024]{2,1,0:T(8,128)S(1)} %all-to-all-done.1.near_ref), channel_id=1, source_target_pairs={{0,1},{1,0},{2,3},{3,2},{4,5},{5,4},{6,7},{7,6},{8,9},{9,8},{10,11... | collective-permute-start | bytes 2359304 | tf_op jit(solution)/shard_map/ppermute | solution.py:250
  45.3 22.9 %all-to-all-start.2 = ((f32[128,4,128]{2,1,0:T(4,128)}), f32[128,4,128]{2,1,0:T(4,128)}, u32[]{:S(2)}, u32[]{:S(2)}) async-start(f32[128,4,128]{2,1,0:T(4,128)} %shard_map.95), calls=%async_computation.2 | async-start | bytes 524288 | tf_op jit(solution)/shard_map/all_to_all | solution.py:251
  58.1 0.8 copy-start.2
  58.9 0.7 copy-start.8
  68.2 1.1 copy-start.3
  69.2 24.4 %copy-start.9 = (f32[160,360]{1,0:T(8,128)S(1)}, f32[160,360]{1,0:T(8,128)}, u32[]{:S(2)}) copy-start(f32[160,360]{1,0:T(8,128)} %copy-done.8) | copy-start | bytes 691204
  71.0 22.6 %collective-permute-start.1 = (f32[160,720]{1,0:T(8,128)S(1)}, f32[160,720]{1,0:T(8,128)S(1)}, u32[]{:S(2)}, u32[]{:S(2)}) collective-permute-start(f32[160,720]{1,0:T(8,128)S(1)} %shard_map.99.near_ref), channel_id=1, source_target_pairs={{0,256},{256,0},{1,257},{257,1},{2,258},{258,2},{3,259},{259,3},{4... | collective-permute-start | bytes 1382408 | tf_op jit(solution)/shard_map/ppermute | solution.py:271
  95.2 38.4 %copy-start.10 = (f32[45]{0:T(128)S(1)}, f32[45]{0:T(128)}, u32[]{:S(2)}) copy-start(f32[45]{0:T(128)} %param.12) | copy-start | bytes 544
  128.1 13.4 %all-to-all-start.4 = ((f32[32,4,128]{2,1,0:T(4,128)}), f32[32,4,128]{2,1,0:T(4,128)S(1)}, u32[]{:S(2)}, u32[]{:S(2)}) async-start(f32[32,4,128]{2,1,0:T(4,128)} %shard_map.102), calls=%async_computation.4 | async-start | bytes 131072 | tf_op jit(solution)/shard_map/all_to_all | solution.py:283

commit v6 on v5

--- a/solution.py
+++ b/solution.py
@@ -245,8 +245,7 @@
         600_000_000,
         scratch=[pltpu.VMEM((256, points), F32)],
     )
-    weight = call(weight_kernel, (slots, spec_weight.transpose(1, 2, 0)), shape(2 * half, degrees), 100_000_000)
-    coeffs, weight, near = lax.optimization_barrier((coeffs, weight, near))
+    coeffs, near = lax.optimization_barrier((coeffs, near))
     far = lax.ppermute(near, ("c",), [(0, 1), (1, 0)])
     coeffs = lax.all_to_all(coeffs, GROUP, 0, 0, tiled=True)
     leg_high, leg_low, sv = call(
@@ -268,6 +267,8 @@
         300_000_000,
         scratch=[pltpu.VMEM((2 * half, 8 * WIDE), F32), pltpu.VMEM((128, 512), F32)],
     )
+    spectra, spec_weight = lax.optimization_barrier((spectra, spec_weight))
+    weight = call(weight_kernel, (slots, spec_weight.transpose(1, 2, 0)), shape(2 * half, degrees), 100_000_000)
     other = lax.ppermute(spectra, ("yh",), [(0, 1), (1, 0)])
     back = call(
         synthesis_kernel,

time: 143 us -> 142 us (level)
    ppermute x1, waiting for transfers between devices: 17.4 us -> 15.8 us  [local(): other = lax.ppermute(spectra, ('yh',), [(0, 1), (1, 0)])]
    unnamed x28 -> x24, local copies, waits for them, and re-layouts: 6.65 us -> 7.2 us
where the time goes in v6:
time: 142 us
  waiting for transfers between devices  51.7 us (36%)
  blocking collectives  44.6 us (31%)
  starting transfers between devices  26.6 us (19%)
  Pallas kernels  10.4 us (7%)
  local copies, waits for them, and re-layouts  7.61 us (5%)
    all_to_all x1, blocking collectives, local(): back = lax.all_to_all(back, GROUP, 0, 0, tiled=True)  32.8 us
    all_to_all x1, waiting for transfers between devices, local(): lax.all_to_all(rows_out.reshape(8, HALF, -1), ('z',), 0, 0, tiled=True)  20.5 us
    ppermute x1, waiting for transfers between devices, local(): other = lax.ppermute(spectra, ('yh',), [(0, 1), (1, 0)])  15.8 us
    all_to_all x1, blocking collectives, local(): rows_out = lax.all_to_all(rows_out, ('c',), 0, 0, tiled=True)  11.8 us
    pallas_call x8, Pallas kernels, call(): pl.pallas_call(kernel, out_shape=out_shapes, in_specs=[smem if i < scalar...  10.4 us
    all_to_all x1, waiting for transfers between devices, local(): coeffs = lax.all_to_all(coeffs, GROUP, 0, 0, tiled=True)  9.65 us
    all_to_all x1, starting transfers between devices, local(): coeffs = lax.all_to_all(coeffs, GROUP, 0, 0, tiled=True)  9.3 us
    unnamed x24, local copies, waits for them, and re-layouts  7.2 us
  transfers between devices with their start and end apart: 5, of which 4 were waited for; matrix products, arithmetic and copies ran while one was open for 0% of the time, Pallas kernels for 5%

profile of v6, /device:TPU:1, one launch (start us, length us, event | category | flops | bytes accessed | tf_op | source)
XLA Modules:
  0.0 141.8 jit_solution(4533753195082291973)
XLA Ops:
  0.6 0.0 copy-start.6
  0.6 1.0 copy-done.6
  1.6 0.0 copy-start.7
  1.6 1.0 copy-done.7
  2.6 0.3 shard_map.96
  2.9 0.0 copy-start
  2.9 0.0 copy-start.1
  2.9 11.8 %all_to_all.25 = f32[2,4,24,1024]{3,2,1,0:T(8,128)} all-to-all(f32[2,4,24,1024]{3,2,1,0:T(8,128)S(1)} %shard_map.96), channel_id=1, replica_groups=mesh['yh'=2,'z'=8,'yl'=4,'x'=4,'c'=2] {'c'}, dimensions={0} | all-to-all | bytes 1572864 | tf_op jit(solution)/shard_map/all_to_all | solution.py:238
  14.7 4.7 %all-to-all-start.1 = ((f32[8,24,1024]{2,1,0:T(8,128)}), f32[8,24,1024]{2,1,0:T(8,128)S(1)}, u32[]{:S(2)}, u32[]{:S(2)}) async-start(f32[8,24,1024]{2,1,0:T(8,128)} %bitcast.3), calls=%async_computation.1 | async-start | bytes 1572864 | tf_op jit(solution)/shard_map/all_to_all | solution.py:239
  19.3 0.0 copy-done
  19.3 0.0 copy-done.1
  19.4 0.0 copy-start.4
  19.4 1.4 copy-done.4
  20.7 0.0 copy-start.9
  20.7 0.0 copy-start.10
  20.7 1.7 %shard_map.95 = f32[128,4,128]{2,1,0:T(4,128)} custom-call(f32[5,45,1440]{2,1,0:T(8,128)S(1)} %copy-done.4, bf16[256,1440]{1,0:T(8,128)(2,1)S(1)} %copy-done, bf16[256,1440]{1,0:T(8,128)(2,1)S(1)} %copy-done.1), custom_call_target="tpu_custom_call" | custom-call | flops 600000000 | bytes 3032704 | tf_op jit(solution)/shard_map/pallas_call | solution.py:205
  22.4 20.5 %all-to-all-done.1.near_ref = f32[8,24,1024]{2,1,0:T(8,128)S(1)} async-done(((f32[8,24,1024]{2,1,0:T(8,128)}), f32[8,24,1024]{2,1,0:T(8,128)S(1)}, u32[]{:S(2)}, u32[]{:S(2)}) %all-to-all-start.1) | async-done | bytes 786464 | tf_op jit(solution)/shard_map/all_to_all | solution.py:239
  42.9 2.4 %collective-permute-start = (f32[8,24,1024]{2,1,0:T(8,128)S(1)}, f32[8,24,1024]{2,1,0:T(8,128)}, u32[]{:S(2)}, u32[]{:S(2)}) collective-permute-start(f32[8,24,1024]{2,1,0:T(8,128)S(1)} %all-to-all-done.1.near_ref), channel_id=1, source_target_pairs={{0,1},{1,0},{2,3},{3,2},{4,5},{5,4},{6,7},{7,6},{8,9},{9,8},{10,11... | collective-permute-start | bytes 2359304 | tf_op jit(solution)/shard_map/ppermute | solution.py:249
  45.3 9.3 %all-to-all-start.2 = ((f32[128,4,128]{2,1,0:T(4,128)}), f32[128,4,128]{2,1,0:T(4,128)S(1)}, u32[]{:S(2)}, u32[]{:S(2)}) async-start(f32[128,4,128]{2,1,0:T(4,128)} %shard_map.95), calls=%async_computation.2 | async-start | bytes 524288 | tf_op jit(solution)/shard_map/all_to_all | solution.py:250
  54.6 0.1 pad_add_fusion.place_ref
  54.7 0.0 copy-done.9
  54.7 0.0 copy-done.10
  54.7 0.0 collective-permute-done.far_ref
  54.7 2.8 %shard_map.97 = (bf16[384,720]{1,0:T(8,128)(2,1)S(1)}, bf16[384,720]{1,0:T(8,128)(2,1)S(1)}, f32[160,360]{1,0:T(8,128)S(1)}) custom-call(s32[3]{0:T(128)S(1)} %pad_add_fusion.place_ref, s32[1,80]{1,0:T(1,128)S(1)} %broadcast_select_fusion.slots_ref, f32[8,24,1024]{2,1,0:T(8,128)S(1)} %all-to-all-done.1.near_ref, f32[8,24,1024]{2,1,0:T(8,128)} %collective-permute-done.far_ref), custom_call_target="tpu_custom_call" | custom-call | flops 100000000 | bytes 2909516 | tf_op jit(solution)/shard_map/pallas_call | solution.py:205
  57.6 0.0 copy-start.2
  57.6 0.8 copy-done.2
  58.4 9.7 %all-to-all-done.2.x_ref = f32[128,4,128]{2,1,0:T(4,128)S(1)} async-done(((f32[128,4,128]{2,1,0:T(4,128)}), f32[128,4,128]{2,1,0:T(4,128)S(1)}, u32[]{:S(2)}, u32[]{:S(2)}) %all-to-all-start.2) | async-done | bytes 262176 | tf_op jit(solution)/shard_map/all_to_all | solution.py:250
  68.1 0.0 copy-start.3
  68.1 1.1 copy-done.3
  69.1 0.8 shard_map.98.near_ref
  69.9 4.8 %collective-permute-start.1 = (f32[160,720]{1,0:T(8,128)S(1)}, f32[160,720]{1,0:T(8,128)S(1)}, u32[]{:S(2)}, u32[]{:S(2)}) collective-permute-start(f32[160,720]{1,0:T(8,128)S(1)} %shard_map.98.near_ref), channel_id=1, source_target_pairs={{0,256},{256,0},{1,257},{257,1},{2,258},{258,2},{3,259},{259,3},{4... | collective-permute-start | bytes 1382408 | tf_op jit(solution)/shard_map/ppermute | solution.py:272
  74.7 0.0 copy-start.5
  74.7 1.2 copy-done.5
  75.9 0.4 shard_map.99.w_ref
  76.3 15.8 %collective-permute-done.1.far_ref = f32[160,720]{1,0:T(8,128)S(1)} collective-permute-done((f32[160,720]{1,0:T(8,128)S(1)}, f32[160,720]{1,0:T(8,128)S(1)}, u32[]{:S(2)}, u32[]{:S(2)}) %collective-permute-start.1) | collective-permute-done | bytes 460832 | tf_op jit(solution)/shard_map/ppermute | solution.py:272
  92.2 1.6 %shard_map.100 = f32[128,8,128]{2,1,0:T(8,128)S(1)} custom-call(s32[3]{0:T(128)S(1)} %pad_add_fusion.place_ref, f32[160,720]{1,0:T(8,128)S(1)} %shard_map.98.near_ref, f32[160,720]{1,0:T(8,128)S(1)} %collective-permute-done.1.far_ref, bf16[384,720]{1,0:T(8,128)(2,1)S(1)} %get-tuple-element.11.lh_ref, bf16[384,720]{1,0:T(8,128)(2,1)S(1)} %copy-done.3, ...), custom_call_target="tpu_custom_call" | custom-call | flops 300000000 | bytes 3243020 | tf_op jit(solution)/shard_map/pallas_call | solution.py:205
  93.7 0.0 copy-start.8
  93.7 32.8 %all_to_all.26.x_ref = f32[128,8,128]{2,1,0:T(8,128)S(1)} all-to-all(f32[128,8,128]{2,1,0:T(8,128)S(1)} %shard_map.100), channel_id=1, replica_groups=mesh['yh'=2,'z'=8,'yl'=4,'x'=4,'c'=2] {'z','yl','x'}, dimensions={0} | all-to-all | bytes 1048576 | tf_op jit(solution)/shard_map/all_to_all | solution.py:281
  126.6 0.8 shard_map.102
  127.4 5.5 %all-to-all-start.4 = ((f32[32,4,128]{2,1,0:T(4,128)}), f32[32,4,128]{2,1,0:T(4,128)S(1)}, u32[]{:S(2)}, u32[]{:S(2)}) async-start(f32[32,4,128]{2,1,0:T(4,128)} %shard_map.102), calls=%async_computation.4 | async-start | bytes 131072 | tf_op jit(solution)/shard_map/all_to_all | solution.py:284
  132.9 0.0 copy-done.8
  132.9 0.1 copy.12.lw_ref
  133.0 2.0 %shard_map.101 = f32[5,45,1440]{2,1,0:T(8,128)} custom-call(f32[128,8,128]{2,1,0:T(8,128)S(1)} %all_to_all.26.x_ref, bf16[256,1440]{1,0:T(8,128)(2,1)S(1)} %copy-done, bf16[256,1440]{1,0:T(8,128)(2,1)S(1)} %copy-done.1, f32[45,1]{1,0:T(8,128)S(1)} %copy.12.lw_ref), custom_call_target="tpu_custom_call" | custom-call | flops 600000000 | bytes 3295028 | tf_op jit(solution)/shard_map/pallas_call | solution.py:205
  135.0 5.7 %all-to-all-done.4 = f32[32,4,128]{2,1,0:T(4,128)S(1)} async-done(((f32[32,4,128]{2,1,0:T(4,128)}), f32[32,4,128]{2,1,0:T(4,128)S(1)}, u32[]{:S(2)}, u32[]{:S(2)}) %all-to-all-start.4) | async-done | bytes 65568 | tf_op jit(solution)/shard_map/all_to_all | solution.py:284
  140.7 0.1 reshape.21
  140.8 0.1 reshape.22
  140.9 0.1 copy.14
  141.1 0.8 copy.15
  (3 shorter events, 0.0 us)
Async XLA Ops:
  0.6 1.0 copy-start.6
  1.6 1.0 copy-start.7
  2.9 16.5 %copy-start = (bf16[256,1440]{1,0:T(8,128)(2,1)S(1)}, bf16[256,1440]{1,0:T(8,128)(2,1)}, u32[]{:S(2)}) copy-start(bf16[256,1440]{1,0:T(8,128)(2,1)} %constant.29.clone.th_ref) | copy-start | bytes 2211844
  2.9 16.5 %copy-start.1 = (bf16[256,1440]{1,0:T(8,128)(2,1)S(1)}, bf16[256,1440]{1,0:T(8,128)(2,1)}, u32[]{:S(2)}) copy-start(bf16[256,1440]{1,0:T(8,128)(2,1)} %constant.30.clone.tl_ref) | copy-start | bytes 2211844
  14.7 28.2 %all-to-all-start.1 = ((f32[8,24,1024]{2,1,0:T(8,128)}), f32[8,24,1024]{2,1,0:T(8,128)S(1)}, u32[]{:S(2)}, u32[]{:S(2)}) async-start(f32[8,24,1024]{2,1,0:T(8,128)} %bitcast.3), calls=%async_computation.1 | async-start | bytes 1572864 | tf_op jit(solution)/shard_map/all_to_all | solution.py:239
  19.4 1.4 copy-start.4
  20.7 34.0 %copy-start.9 = (s32[1,80]{1,0:T(1,128)S(1)}, s32[1,80]{1,0:T(1,128)}, u32[]{:S(2)}) copy-start(s32[1,80]{1,0:T(1,128)} %constant.35) | copy-start | bytes 964
  20.7 34.0 %copy-start.10 = (s32[1,80]{1,0:T(1,128)S(1)}, s32[1,80]{1,0:T(1,128)}, u32[]{:S(2)}) copy-start(s32[1,80]{1,0:T(1,128)} %constant.36) | copy-start | bytes 964
  42.9 11.8 %collective-permute-start = (f32[8,24,1024]{2,1,0:T(8,128)S(1)}, f32[8,24,1024]{2,1,0:T(8,128)}, u32[]{:S(2)}, u32[]{:S(2)}) collective-permute-start(f32[8,24,1024]{2,1,0:T(8,128)S(1)} %all-to-all-done.1.near_ref), channel_id=1, source_target_pairs={{0,1},{1,0},{2,3},{3,2},{4,5},{5,4},{6,7},{7,6},{8,9},{9,8},{10,11... | collective-permute-start | bytes 2359304 | tf_op jit(solution)/shard_map/ppermute | solution.py:249
  45.3 22.7 %all-to-all-start.2 = ((f32[128,4,128]{2,1,0:T(4,128)}), f32[128,4,128]{2,1,0:T(4,128)S(1)}, u32[]{:S(2)}, u32[]{:S(2)}) async-start(f32[128,4,128]{2,1,0:T(4,128)} %shard_map.95), calls=%async_computation.2 | async-start | bytes 524288 | tf_op jit(solution)/shard_map/all_to_all | solution.py:250
  57.6 0.8 copy-start.2
  68.1 1.1 copy-start.3
  69.9 22.3 %collective-permute-start.1 = (f32[160,720]{1,0:T(8,128)S(1)}, f32[160,720]{1,0:T(8,128)S(1)}, u32[]{:S(2)}, u32[]{:S(2)}) collective-permute-start(f32[160,720]{1,0:T(8,128)S(1)} %shard_map.98.near_ref), channel_id=1, source_target_pairs={{0,256},{256,0},{1,257},{257,1},{2,258},{258,2},{3,259},{259,3},{4... | collective-permute-start | bytes 1382408 | tf_op jit(solution)/shard_map/ppermute | solution.py:272
  74.7 1.2 copy-start.5
  93.7 39.1 %copy-start.8 = (f32[45]{0:T(128)S(1)}, f32[45]{0:T(128)}, u32[]{:S(2)}) copy-start(f32[45]{0:T(128)} %param.12) | copy-start | bytes 544
  127.4 13.3 %all-to-all-start.4 = ((f32[32,4,128]{2,1,0:T(4,128)}), f32[32,4,128]{2,1,0:T(4,128)S(1)}, u32[]{:S(2)}, u32[]{:S(2)}) async-start(f32[32,4,128]{2,1,0:T(4,128)} %shard_map.102), calls=%async_computation.4 | async-start | bytes 131072 | tf_op jit(solution)/shard_map/all_to_all | solution.py:284

commit v7 on v6

--- a/solution.py
+++ b/solution.py
@@ -134,6 +134,19 @@
             sv_ref[to, at + TOP : at + rows] = mine[:, src + HALF : src + HALF + rows - TOP]
 
 
+def moves(half):
+    at = 5 * 2 * half
+    out = [(slice(0, half), slice(640, 720), slice(at, at + half), slice(0, 80))]
+    out.append((slice(half, 2 * half), slice(640, 688), slice(at, at + half), slice(80, 128)))
+    for i, low in enumerate(range(0, half, 24)):
+        n = min(24, half - low)
+        rows = slice(half + low, half + low + n)
+        out.append((rows, slice(688, 720), slice(at + half, at + half + n), slice(32 * i, 32 * i + 32)))
+    for k in range(5):
+        out.append((slice(0, 2 * half), slice(128 * k, 128 * k + 128), slice(2 * half * k, 2 * half * (k + 1)), slice(0, 128)))
+    return out
+
+
 def analysis_kernel(x_ref, lh_ref, ll_ref, out_ref, ct, tmp):
     for k in range(4):
         tmp[:, k * 128 : (k + 1) * 128] = x_ref[:, k, :]
@@ -146,14 +159,19 @@
     ch, cl = two(ct[...])
     n = ch.shape[0]
     both = dot(jnp.concatenate([ch, cl], axis=0), lh_ref[...], NN)
-    out_ref[...] = both[:n] + both[n:] + dot(ch, ll_ref[...], NN)
-
-
-def synthesis_kernel(place_ref, near_ref, far_ref, lh_ref, ll_ref, sv_ref, w_ref, out_ref, back):
+    spec = both[:n] + both[n:] + dot(ch, ll_ref[...], NN)
+    out_ref[out_ref.shape[0] - 24 :, :] = jnp.zeros((24, 128), F32)
+    for rows, lanes, to, there in moves(n // 2):
+        out_ref[to, there] = spec[rows, lanes]
+
+
+def synthesis_kernel(place_ref, near_ref, far_ref, lh_ref, ll_ref, sv_ref, w_ref, out_ref, back, full):
     half, degrees = w_ref.shape[0] // 2, w_ref.shape[1]
     n, rows = 2 * half, degrees // 16
     back[...] = jnp.zeros_like(back)
-    spec = near_ref[...] + far_ref[...]
+    for to, there, at, lanes in moves(half):
+        full[to, there] = near_ref[at, lanes] + far_ref[at, lanes]
+    spec = full[...]
     g, h = spec[:half], spec[half:]
     u, v = w_ref[:half, :], w_ref[half:, :]
     twice = jnp.where(place_ref[2] == 1, 1.0, 2.0).astype(F32)
@@ -263,7 +281,7 @@
     spectra = call(
         analysis_kernel,
         (coeffs, leg_high, leg_low),
-        shape(2 * half, degrees),
+        shape(11 * half + 24, 128),
         300_000_000,
         scratch=[pltpu.VMEM((2 * half, 8 * WIDE), F32), pltpu.VMEM((128, 512), F32)],
     )
@@ -275,7 +293,7 @@
         (place, spectra, other, leg_high, leg_low, sv, weight),
         shape(128, 8, 128),
         300_000_000,
-        scratch=[pltpu.VMEM((128, 1024), F32)],
+        scratch=[pltpu.VMEM((128, 1024), F32), pltpu.VMEM((2 * half, degrees), F32)],
         scalars=1,
     )
     back = lax.all_to_all(back, GROUP, 0, 0, tiled=True)

time: 142 us -> 141 us (level)
  waiting for transfers between devices: 51.7 us -> 50 us
    ppermute x1, waiting for transfers between devices: 15.8 us -> 14.1 us  [local(): other = lax.ppermute(spectra, ('yh',), [(0, 1), (1, 0)])]
where the time goes in v7:
time: 141 us
  waiting for transfers between devices  50 us (35%)
  blocking collectives  45.1 us (32%)
  starting transfers between devices  26.6 us (19%)
  Pallas kernels  10.4 us (7%)
  local copies, waits for them, and re-layouts  7.61 us (5%)
    all_to_all x1, blocking collectives, local(): back = lax.all_to_all(back, GROUP, 0, 0, tiled=True)  33.3 us
    all_to_all x1, waiting for transfers between devices, local(): lax.all_to_all(rows_out.reshape(8, HALF, -1), ('z',), 0, 0, tiled=True)  20.5 us
    ppermute x1, waiting for transfers between devices, local(): other = lax.ppermute(spectra, ('yh',), [(0, 1), (1, 0)])  14.1 us
    all_to_all x1, blocking collectives, local(): rows_out = lax.all_to_all(rows_out, ('c',), 0, 0, tiled=True)  11.8 us
    pallas_call x8, Pallas kernels, call(): pl.pallas_call(kernel, out_shape=out_shapes, in_specs=[smem if i < scalar...  10.4 us
    all_to_all x1, waiting for transfers between devices, local(): coeffs = lax.all_to_all(coeffs, GROUP, 0, 0, tiled=True)  9.65 us
    all_to_all x1, starting transfers between devices, local(): coeffs = lax.all_to_all(coeffs, GROUP, 0, 0, tiled=True)  9.3 us
    unnamed x24, local copies, waits for them, and re-layouts  7.2 us
  transfers between devices with their start and end apart: 5, of which 4 were waited for; matrix products, arithmetic and copies ran while one was open for 0% of the time, Pallas kernels for 5%

profile of v7, /device:TPU:1, one launch (start us, length us, event | category | flops | bytes accessed | tf_op | source)
XLA Modules:
  0.0 140.7 jit_solution(5915690618014763417)
XLA Ops:
  0.6 0.0 copy-start.6
  0.6 1.0 copy-done.6
  1.6 0.0 copy-start.7
  1.6 1.0 copy-done.7
  2.6 0.3 shard_map.96
  2.9 0.0 copy-start
  2.9 0.0 copy-start.1
  2.9 11.8 %all_to_all.25 = f32[2,4,24,1024]{3,2,1,0:T(8,128)} all-to-all(f32[2,4,24,1024]{3,2,1,0:T(8,128)S(1)} %shard_map.96), channel_id=1, replica_groups=mesh['yh'=2,'z'=8,'yl'=4,'x'=4,'c'=2] {'c'}, dimensions={0} | all-to-all | bytes 1572864 | tf_op jit(solution)/shard_map/all_to_all | solution.py:256
  14.7 4.7 %all-to-all-start.1 = ((f32[8,24,1024]{2,1,0:T(8,128)}), f32[8,24,1024]{2,1,0:T(8,128)S(1)}, u32[]{:S(2)}, u32[]{:S(2)}) async-start(f32[8,24,1024]{2,1,0:T(8,128)} %bitcast.3), calls=%async_computation.1 | async-start | bytes 1572864 | tf_op jit(solution)/shard_map/all_to_all | solution.py:257
  19.3 0.0 copy-done
  19.3 0.0 copy-done.1
  19.4 0.0 copy-start.4
  19.4 1.4 copy-done.4
  20.7 0.0 copy-start.9
  20.7 0.0 copy-start.10
  20.7 1.7 %shard_map.95 = f32[128,4,128]{2,1,0:T(4,128)} custom-call(f32[5,45,1440]{2,1,0:T(8,128)S(1)} %copy-done.4, bf16[256,1440]{1,0:T(8,128)(2,1)S(1)} %copy-done, bf16[256,1440]{1,0:T(8,128)(2,1)S(1)} %copy-done.1), custom_call_target="tpu_custom_call" | custom-call | flops 600000000 | bytes 3032704 | tf_op jit(solution)/shard_map/pallas_call | solution.py:223
  22.4 20.5 %all-to-all-done.1.near_ref = f32[8,24,1024]{2,1,0:T(8,128)S(1)} async-done(((f32[8,24,1024]{2,1,0:T(8,128)}), f32[8,24,1024]{2,1,0:T(8,128)S(1)}, u32[]{:S(2)}, u32[]{:S(2)}) %all-to-all-start.1) | async-done | bytes 786464 | tf_op jit(solution)/shard_map/all_to_all | solution.py:257
  42.9 2.4 %collective-permute-start = (f32[8,24,1024]{2,1,0:T(8,128)S(1)}, f32[8,24,1024]{2,1,0:T(8,128)}, u32[]{:S(2)}, u32[]{:S(2)}) collective-permute-start(f32[8,24,1024]{2,1,0:T(8,128)S(1)} %all-to-all-done.1.near_ref), channel_id=1, source_target_pairs={{0,1},{1,0},{2,3},{3,2},{4,5},{5,4},{6,7},{7,6},{8,9},{9,8},{10,11... | collective-permute-start | bytes 2359304 | tf_op jit(solution)/shard_map/ppermute | solution.py:267
  45.3 9.3 %all-to-all-start.2 = ((f32[128,4,128]{2,1,0:T(4,128)}), f32[128,4,128]{2,1,0:T(4,128)S(1)}, u32[]{:S(2)}, u32[]{:S(2)}) async-start(f32[128,4,128]{2,1,0:T(4,128)} %shard_map.95), calls=%async_computation.2 | async-start | bytes 524288 | tf_op jit(solution)/shard_map/all_to_all | solution.py:268
  54.6 0.1 pad_add_fusion.place_ref
  54.7 0.0 copy-done.9
  54.7 0.0 copy-done.10
  54.7 0.0 collective-permute-done.far_ref
  54.7 2.8 %shard_map.97 = (bf16[384,720]{1,0:T(8,128)(2,1)S(1)}, bf16[384,720]{1,0:T(8,128)(2,1)S(1)}, f32[160,360]{1,0:T(8,128)S(1)}) custom-call(s32[3]{0:T(128)S(1)} %pad_add_fusion.place_ref, s32[1,80]{1,0:T(1,128)S(1)} %broadcast_select_fusion.slots_ref, f32[8,24,1024]{2,1,0:T(8,128)S(1)} %all-to-all-done.1.near_ref, f32[8,24,1024]{2,1,0:T(8,128)} %collective-permute-done.far_ref), custom_call_target="tpu_custom_call" | custom-call | flops 100000000 | bytes 2909516 | tf_op jit(solution)/shard_map/pallas_call | solution.py:223
  57.6 0.0 copy-start.2
  57.6 0.8 copy-done.2
  58.4 9.7 %all-to-all-done.2.x_ref = f32[128,4,128]{2,1,0:T(4,128)S(1)} async-done(((f32[128,4,128]{2,1,0:T(4,128)}), f32[128,4,128]{2,1,0:T(4,128)S(1)}, u32[]{:S(2)}, u32[]{:S(2)}) %all-to-all-start.2) | async-done | bytes 262176 | tf_op jit(solution)/shard_map/all_to_all | solution.py:268
  68.1 0.0 copy-start.3
  68.1 1.1 copy-done.3
  69.1 0.8 shard_map.98.near_ref
  70.0 4.8 %collective-permute-start.1 = (f32[904,128]{1,0:T(8,128)S(1)}, f32[904,128]{1,0:T(8,128)S(1)}, u32[]{:S(2)}, u32[]{:S(2)}) collective-permute-start(f32[904,128]{1,0:T(8,128)S(1)} %shard_map.98.near_ref), channel_id=1, source_target_pairs={{0,256},{256,0},{1,257},{257,1},{2,258},{258,2},{3,259},{259,3},{4... | collective-permute-start | bytes 1388552 | tf_op jit(solution)/shard_map/ppermute | solution.py:290
  74.7 0.0 copy-start.5
  74.7 1.2 copy-done.5
  75.9 0.4 shard_map.99.w_ref
  76.4 14.1 %collective-permute-done.1.far_ref = f32[904,128]{1,0:T(8,128)S(1)} collective-permute-done((f32[904,128]{1,0:T(8,128)S(1)}, f32[904,128]{1,0:T(8,128)S(1)}, u32[]{:S(2)}, u32[]{:S(2)}) %collective-permute-start.1) | collective-permute-done | bytes 462880 | tf_op jit(solution)/shard_map/ppermute | solution.py:290
  90.5 1.6 %shard_map.100 = f32[128,8,128]{2,1,0:T(8,128)S(1)} custom-call(s32[3]{0:T(128)S(1)} %pad_add_fusion.place_ref, f32[904,128]{1,0:T(8,128)S(1)} %shard_map.98.near_ref, f32[904,128]{1,0:T(8,128)S(1)} %collective-permute-done.1.far_ref, bf16[384,720]{1,0:T(8,128)(2,1)S(1)} %get-tuple-element.11.lh_ref, bf16[384,720]{1,0:T(8,128)(2,1)S(1)} %copy-done.3, ...), custom_call_target="tpu_custom_call" | custom-call | flops 300000000 | bytes 3247116 | tf_op jit(solution)/shard_map/pallas_call | solution.py:223
  92.1 0.0 copy-start.8
  92.1 33.3 %all_to_all.26.x_ref = f32[128,8,128]{2,1,0:T(8,128)S(1)} all-to-all(f32[128,8,128]{2,1,0:T(8,128)S(1)} %shard_map.100), channel_id=1, replica_groups=mesh['yh'=2,'z'=8,'yl'=4,'x'=4,'c'=2] {'z','yl','x'}, dimensions={0} | all-to-all | bytes 1048576 | tf_op jit(solution)/shard_map/all_to_all | solution.py:299
  125.4 0.8 shard_map.102
  126.2 5.5 %all-to-all-start.4 = ((f32[32,4,128]{2,1,0:T(4,128)}), f32[32,4,128]{2,1,0:T(4,128)S(1)}, u32[]{:S(2)}, u32[]{:S(2)}) async-start(f32[32,4,128]{2,1,0:T(4,128)} %shard_map.102), calls=%async_computation.4 | async-start | bytes 131072 | tf_op jit(solution)/shard_map/all_to_all | solution.py:302
  131.7 0.0 copy-done.8
  131.7 0.1 copy.12.lw_ref
  131.8 2.0 %shard_map.101 = f32[5,45,1440]{2,1,0:T(8,128)} custom-call(f32[128,8,128]{2,1,0:T(8,128)S(1)} %all_to_all.26.x_ref, bf16[256,1440]{1,0:T(8,128)(2,1)S(1)} %copy-done, bf16[256,1440]{1,0:T(8,128)(2,1)S(1)} %copy-done.1, f32[45,1]{1,0:T(8,128)S(1)} %copy.12.lw_ref), custom_call_target="tpu_custom_call" | custom-call | flops 600000000 | bytes 3295028 | tf_op jit(solution)/shard_map/pallas_call | solution.py:223
  133.8 5.7 %all-to-all-done.4 = f32[32,4,128]{2,1,0:T(4,128)S(1)} async-done(((f32[32,4,128]{2,1,0:T(4,128)}), f32[32,4,128]{2,1,0:T(4,128)S(1)}, u32[]{:S(2)}, u32[]{:S(2)}) %all-to-all-start.4) | async-done | bytes 65568 | tf_op jit(solution)/shard_map/all_to_all | solution.py:302
  139.5 0.1 reshape.21
  139.6 0.1 reshape.22
  139.8 0.1 copy.14
  139.9 0.8 copy.15
  (3 shorter events, 0.0 us)
Async XLA Ops:
  0.6 1.0 copy-start.6
  1.6 1.0 copy-start.7
  2.9 16.5 %copy-start = (bf16[256,1440]{1,0:T(8,128)(2,1)S(1)}, bf16[256,1440]{1,0:T(8,128)(2,1)}, u32[]{:S(2)}) copy-start(bf16[256,1440]{1,0:T(8,128)(2,1)} %constant.29.clone.th_ref) | copy-start | bytes 2211844
  2.9 16.5 %copy-start.1 = (bf16[256,1440]{1,0:T(8,128)(2,1)S(1)}, bf16[256,1440]{1,0:T(8,128)(2,1)}, u32[]{:S(2)}) copy-start(bf16[256,1440]{1,0:T(8,128)(2,1)} %constant.30.clone.tl_ref) | copy-start | bytes 2211844
  14.7 28.2 %all-to-all-start.1 = ((f32[8,24,1024]{2,1,0:T(8,128)}), f32[8,24,1024]{2,1,0:T(8,128)S(1)}, u32[]{:S(2)}, u32[]{:S(2)}) async-start(f32[8,24,1024]{2,1,0:T(8,128)} %bitcast.3), calls=%async_computation.1 | async-start | bytes 1572864 | tf_op jit(solution)/shard_map/all_to_all | solution.py:257
  19.4 1.4 copy-start.4
  20.7 34.0 %copy-start.9 = (s32[1,80]{1,0:T(1,128)S(1)}, s32[1,80]{1,0:T(1,128)}, u32[]{:S(2)}) copy-start(s32[1,80]{1,0:T(1,128)} %constant.35) | copy-start | bytes 964
  20.7 34.0 %copy-start.10 = (s32[1,80]{1,0:T(1,128)S(1)}, s32[1,80]{1,0:T(1,128)}, u32[]{:S(2)}) copy-start(s32[1,80]{1,0:T(1,128)} %constant.36) | copy-start | bytes 964
  42.9 11.8 %collective-permute-start = (f32[8,24,1024]{2,1,0:T(8,128)S(1)}, f32[8,24,1024]{2,1,0:T(8,128)}, u32[]{:S(2)}, u32[]{:S(2)}) collective-permute-start(f32[8,24,1024]{2,1,0:T(8,128)S(1)} %all-to-all-done.1.near_ref), channel_id=1, source_target_pairs={{0,1},{1,0},{2,3},{3,2},{4,5},{5,4},{6,7},{7,6},{8,9},{9,8},{10,11... | collective-permute-start | bytes 2359304 | tf_op jit(solution)/shard_map/ppermute | solution.py:267
  45.3 22.7 %all-to-all-start.2 = ((f32[128,4,128]{2,1,0:T(4,128)}), f32[128,4,128]{2,1,0:T(4,128)S(1)}, u32[]{:S(2)}, u32[]{:S(2)}) async-start(f32[128,4,128]{2,1,0:T(4,128)} %shard_map.95), calls=%async_computation.2 | async-start | bytes 524288 | tf_op jit(solution)/shard_map/all_to_all | solution.py:268
  57.6 0.8 copy-start.2
  68.1 1.1 copy-start.3
  70.0 20.6 %collective-permute-start.1 = (f32[904,128]{1,0:T(8,128)S(1)}, f32[904,128]{1,0:T(8,128)S(1)}, u32[]{:S(2)}, u32[]{:S(2)}) collective-permute-start(f32[904,128]{1,0:T(8,128)S(1)} %shard_map.98.near_ref), channel_id=1, source_target_pairs={{0,256},{256,0},{1,257},{257,1},{2,258},{258,2},{3,259},{259,3},{4... | collective-permute-start | bytes 1388552 | tf_op jit(solution)/shard_map/ppermute | solution.py:290
  74.7 1.2 copy-start.5
  92.1 39.6 %copy-start.8 = (f32[45]{0:T(128)S(1)}, f32[45]{0:T(128)}, u32[]{:S(2)}) copy-start(f32[45]{0:T(128)} %param.12) | copy-start | bytes 544
  126.2 13.3 %all-to-all-start.4 = ((f32[32,4,128]{2,1,0:T(4,128)}), f32[32,4,128]{2,1,0:T(4,128)S(1)}, u32[]{:S(2)}, u32[]{:S(2)}) async-start(f32[32,4,128]{2,1,0:T(4,128)} %shard_map.102), calls=%async_computation.4 | async-start | bytes 131072 | tf_op jit(solution)/shard_map/all_to_all | solution.py:302
